TPU v7x, 512 devices: a whole 4x4x16 slice. The times are simulated.
512 devices in a mesh: site: 16 (over z), bond: 32 (over y, x, core).
Axes of the slice: x: 4, y: 4, z: 16, core: 2. Of those that a mesh axis runs over, the one named last changes fastest.
Arguments:
- site_tensor: float32 [16, 4, 3072, 3072], P('site', None, 'bond'), may hold values from -0.21875 to 0.21875
- panels: float32 [16, 3072, 128], P('site', 'bond'), may hold values from -6 to 6
- fresh: float32 [1, 3072, 128], P(None, 'bond'), may hold values from -6 to 6
- outcomes: int32 [16, 2, 128], P('site'), may hold values from 0 to 3, as said below
Outputs:
- carried: float32 [16, 2, 3072, 128], P('site', None, 'bond')
Inputs may be any that keep to these rules, and one draw needn't show every extreme that they name: `outcomes`: at each site and tick, every outcome is taken by at most 48 samples, and some outcome by exactly 48.
All inputs are finite; a program needn't handle non-finite values.
Results may differ from a plain program's by a relative error of at most 0.0001.
Values sent between devices are 32-bit elements; how exact they have to be, the bound alone decides.
No kernel may reach another device: no remote copies, remote signals or barrier semaphores. Data moves between devices by JAX's collectives and lax.ppermute only.
A program may use at most 64 MiB of HBM per device.

v0:
```python
import jax
import jax.numpy as jnp
from jax import lax
from jax.sharding import PartitionSpec as P

TICKS = 2


def from_behind(value, axis, steps):
    count = lax.axis_size(axis)
    initial, last = (max(0, -steps), min(count, count - steps))
    return lax.ppermute(value, axis, [(source, source + steps) for source in range(initial, last)])


def contribute(tensor, vectors, selected):
    outcome_count = tensor.shape[0]
    chosen = (selected[None, :] == jnp.arange(outcome_count, dtype=jnp.int32)[:, None]).astype(
        jnp.float32
    )
    products = lax.dot_general(
        tensor,
        vectors,
        (((1,), (0,)), ((), ())),
        precision=lax.Precision.HIGHEST,
        preferred_element_type=jnp.float32,
    )
    return jnp.sum(products * chosen[:, None, :], axis=0)


def advance(tensor, vectors, selected):
    rows_local = tensor.shape[1]
    complete = contribute(tensor, vectors, selected)
    summed = lax.psum(complete, "bond")
    bond_index = lax.axis_index("bond")
    return lax.dynamic_slice_in_dim(summed, bond_index * rows_local, rows_local, 0)


def on_device(site_tensor, panels, fresh, outcomes):
    tensor = site_tensor[0]
    current = panels[0]
    results = []
    for tick_index in range(TICKS):
        produced = advance(tensor, current, outcomes[0, tick_index])
        results.append(produced)
        if tick_index + 1 < TICKS:
            passed = from_behind(produced, "site", 1)
            current = jnp.where(lax.axis_index("site") == 0, fresh[tick_index], passed)
    return jnp.stack(results, 0)[None]


def solution(mesh):
    placed = (
        P("site", None, "bond", None),
        P("site", "bond", None),
        P(None, "bond", None),
        P("site", None, None),
    )
    return jax.shard_map(
        on_device,
        mesh=mesh,
        in_specs=placed,
        out_specs=P("site", None, "bond", None),
        check_vma=False,
    )
```

profile of v0, /device:TPU:6, one launch (start us, length us, event | category | flops | bytes accessed | tf_op | source)
XLA Modules:
  0.0 324.4 jit_solution(2614767855735934217)
XLA Ops:
  6.5 0.0 copy-start
  6.5 0.0 copy-start.1
  6.5 0.0 all-reduce.3.cloned.1.call-start
  6.5 0.8 slice_bitcast_fusion.1
  7.3 0.1 copy-done
  7.4 13.1 %multiply_reduce_fusion = f32[3072,128]{1,0:T(8,128)} fusion(f32[1,4,96,3072]{3,2,1,0:T(8,128)} %param.4, f32[4,128]{1,0:T(4,128)S(1)} %fusion.6, f32[1,96,128]{2,1,0:T(8,128)S(1)} %copy-done), kind=kOutput, calls=%fused_computation.2 | convolution fusion | flops 1814691840 | bytes 6342656 | tf_op jit(solution)/shard_map/dot_general | solution.py:20
  20.4 0.0 all-reduce.3.cloned.1.call-update
  20.4 0.0 all-reduce.5.cloned.1.call-start
  20.5 142.2 %all-reduce.3.cloned.1.call-done = f32[3072,128]{1,0:T(8,128)} async-done(((f32[3072,128]{1,0:T(8,128)}), f32[3072,128]{1,0:T(8,128)}) %all-reduce.3.cloned.1.call-update) | async-done | bytes 1572880 | tf_op jit(solution)/shard_map/psum | solution.py:33
  162.7 0.8 constant_dynamic-slice_fusion.1
  163.5 3.4 %collective-permute-start = (f32[96,128]{1,0:T(8,128)S(1)}, f32[96,128]{1,0:T(8,128)S(1)}, u32[]{:S(2)}, u32[]{:S(2)}) collective-permute-start(f32[96,128]{1,0:T(8,128)S(1)} %constant_dynamic-slice_fusion.1), channel_id=1, source_target_pairs={{0,32},{32,64},{64,96},{96,128},{128,160},{160,192},{192,224},{224... | collective-permute-start | bytes 147464 | tf_op jit(solution)/shard_map/ppermute | solution.py:12
  167.0 1.7 collective-permute-done
  168.7 0.0 copy-done.1
  168.7 8.6 %fusion = f32[3072,128]{0,1:T(8,128)} fusion(f32[1,4,96,3072]{3,2,1,0:T(8,128)} %param.4, f32[4,128]{1,0:T(4,128)S(1)} %fusion.7, f32[96,128]{1,0:T(8,128)S(1)} %collective-permute-done, f32[1,96,128]{2,1,0:T(8,128)S(1)} %copy-done.1, pred[]{:T(512)S(6)} %eq.45), kind=kOutput, calls=%fused_computation.1 | convolution fusion | flops 1814704128 | bytes 6391809 | tf_op jit(solution)/shard_map/dot_general | solution.py:20
  177.3 0.0 all-reduce.5.cloned.1.call-update
  177.4 0.8 fusion.8
  178.2 137.6 %all-reduce.5.cloned.1.call-done = f32[3072,128]{0,1:T(8,128)} async-done(((f32[3072,128]{0,1:T(8,128)}), f32[3072,128]{0,1:T(8,128)}) %all-reduce.5.cloned.1.call-update) | async-done | bytes 1572880 | tf_op jit(solution)/shard_map/psum | solution.py:33
  315.8 1.0 constant_dynamic-slice_fusion
  316.8 0.1 copy.5
  316.9 0.7 maximum_bitcast_fusion
  (2 shorter events, 0.0 us)
Async XLA Ops:
  6.5 0.8 copy-start
  6.5 162.2 %copy-start.1 = (f32[1,96,128]{2,1,0:T(8,128)S(1)}, f32[1,96,128]{2,1,0:T(8,128)}, u32[]{:S(2)}) copy-start(f32[1,96,128]{2,1,0:T(8,128)} %param.6) | copy-start | bytes 147460
  6.5 156.2 %all-reduce.3.cloned.1.call-start = ((), (), s32[]{:S(2)}) async-start(), calls=%async_computation | async-start | bytes 3145728 | tf_op jit(solution)/shard_map/psum | solution.py:33
  20.4 295.4 %all-reduce.5.cloned.1.call-start = ((), (), s32[]{:S(2)}) async-start(), calls=%async_computation.1 | async-start | bytes 3145728 | tf_op jit(solution)/shard_map/psum | solution.py:33
  163.5 5.2 %collective-permute-start = (f32[96,128]{1,0:T(8,128)S(1)}, f32[96,128]{1,0:T(8,128)S(1)}, u32[]{:S(2)}, u32[]{:S(2)}) collective-permute-start(f32[96,128]{1,0:T(8,128)S(1)} %constant_dynamic-slice_fusion.1), channel_id=1, source_target_pairs={{0,32},{32,64},{64,96},{96,128},{128,160},{160,192},{192,224},{224... | collective-permute-start | bytes 147464 | tf_op jit(solution)/shard_map/ppermute | solution.py:12
Sparse Core Ops, SparseCore 0:
  20.6 142.1 all-reduce.2
  177.5 138.2 all-reduce.4
where the time goes:
time: 325 us; the launch traced here: 324 us
  waiting for transfers between devices  282 us (87%)
  matrix products  21.7 us (7%)
  between operations  13.4 us (4%)
  local copies, waits for them, and re-layouts  3.5 us (1%)
  starting transfers between devices  3.49 us (1%)
    psum x2, waiting for transfers between devices, advance(): summed = lax.psum(complete, 'bond')  280 us
    dot_general x2, matrix products, contribute(): lax.dot_general(tensor, vectors, (((1,), (0,)), ((), ())), precision=lax....  21.7 us
  transfers between devices with their start and end apart: 3, of which 3 were waited for; matrix products, arithmetic and copies ran while one was open for 0% of the time, Pallas kernels for 0%

commit v1 on v0

v1 whole, which is shorter than its diff:
```python
import jax
import jax.numpy as jnp
from jax import lax
from jax.sharding import Mesh, PartitionSpec as P

TICKS = 2
CHIPS = ("y", "x")
BOND = ("y", "x", "core")


def contribute(tensor, vectors, selected):
    outcome_count, rows, columns = tensor.shape
    chosen = selected[None, :] == jnp.arange(outcome_count, dtype=jnp.int32)[:, None]
    masked = jnp.where(chosen[:, None, :], vectors[None], 0.0)
    return lax.dot_general(
        tensor.reshape(outcome_count * rows, columns),
        masked.reshape(outcome_count * rows, -1),
        (((0,), (0,)), ((), ())),
        precision=lax.Precision.HIGH,
        preferred_element_type=jnp.float32,
    )


def scatter_sum(partial, rows, chips):
    core = lax.axis_index("core")
    blocks = partial.reshape(chips, 2, rows, partial.shape[-1])
    kept = lax.dynamic_index_in_dim(blocks, core, 1, keepdims=False)
    sent = lax.dynamic_index_in_dim(blocks, 1 - core, 1, keepdims=False)
    paired = kept + lax.ppermute(sent, "core", [(0, 1), (1, 0)])
    return lax.all_to_all(paired, CHIPS, 0, 0, tiled=True).sum(0)


def on_device(site_tensor, panels, fresh, outcomes):
    tensor = site_tensor[0]
    rows = tensor.shape[1]
    chips = tensor.shape[2] // rows // 2
    sites = lax.axis_size("site")
    current = panels[0]
    results = []
    for tick in range(TICKS):
        partial = contribute(tensor, current, outcomes[0, tick])
        produced = scatter_sum(partial, rows, chips)
        results.append(produced)
        if tick + 1 < TICKS:
            passed = lax.ppermute(produced, "site", [(i, i + 1) for i in range(sites - 1)])
            current = jnp.where(lax.axis_index("site") == 0, fresh[tick], passed)
    return jnp.stack(results, 0)[None]


def solution(mesh):
    sites, bonds = mesh.devices.shape
    side = round((bonds // 2) ** 0.5)
    split = Mesh(mesh.devices.reshape(sites, side, side, 2), ("site", "y", "x", "core"))
    placed = (
        P("site", None, BOND, None),
        P("site", BOND, None),
        P(None, BOND, None),
        P("site", None, None),
    )
    return jax.shard_map(
        on_device,
        mesh=split,
        in_specs=placed,
        out_specs=P("site", None, BOND, None),
        check_vma=False,
    )
```

time: 325 us -> 66.7 us (0.21)
  the two profiles are of different devices: /device:TPU:6 before, /device:TPU:128 now
where the time goes in v1:
time: 66.7 us; the launch traced here: 66.3 us
  blocking collectives  39.2 us (59%)
  matrix products  7.93 us (12%)
  waiting for transfers between devices  7.84 us (12%)
  starting transfers between devices  7.67 us (11%)
  local copies, waits for them, and re-layouts  1.81 us (3%)
  other arithmetic  1.77 us (3%)
    all_to_all x2, blocking collectives, scatter_sum(): return lax.all_to_all(paired, CHIPS, 0, 0, tiled=True).sum(0)  39.2 us
    dot_general x2, matrix products, contribute(): lax.dot_general(tensor.reshape(outcome_count * rows, columns), masked.res...  7.93 us
    ppermute x2, waiting for transfers between devices, scatter_sum(): paired = kept + lax.ppermute(sent, 'core', [(0, 1), (1, 0)])  4.5 us
    ppermute x2, starting transfers between devices, scatter_sum(): paired = kept + lax.ppermute(sent, 'core', [(0, 1), (1, 0)])  3.84 us
    ppermute x1, starting transfers between devices, on_device(): lax.ppermute(produced, 'site', [(i, i + 1) for i in range(sites - 1)])  3.83 us
    ppermute x1, waiting for transfers between devices, on_device(): lax.ppermute(produced, 'site', [(i, i + 1) for i in range(sites - 1)])  3.34 us
  transfers between devices with their start and end apart: 3, of which 3 were waited for; matrix products, arithmetic and copies ran while one was open for 0% of the time, Pallas kernels for 0%

profile of v1, /device:TPU:128, one launch (start us, length us, event | category | flops | bytes accessed | tf_op | source)
XLA Modules:
  0.0 66.3 jit_solution(6744098401971813485)
XLA Ops:
  0.0 0.8 %slice_bitcast_fusion = (s32[128]{0:T(128)S(1)}, s32[128]{0:T(128)S(1)}) fusion(s32[1,2,128]{2,1,0:T(2,128)} %param.7), kind=kLoop, calls=%fused_computation.12 | loop fusion | bytes 2048 | tf_op jit(solution)/shard_map/eq | solution.py:13
  0.8 0.8 %broadcast_select_fusion.1 = f32[4,96,128]{2,1,0:T(8,128)S(1)} fusion(f32[96,128]{1,0:T(8,128)} %bitcast.42, pred[4,128]{1,0:T(4,128)(4,1)S(1)} %iota_compare_fusion.1), kind=kLoop, calls=%fused_computation.8 | loop fusion | flops 49152 | bytes 246272 | tf_op jit(solution)/shard_map/jit(_where)/select_n | solution.py:14
  1.6 4.0 %convolution_bitcast_fusion.1 = f32[3072,128]{0,1:T(8,128)S(1)} fusion(f32[384,128]{1,0:T(8,128)S(1)} %bitcast.39, f32[384,3072]{1,0:T(8,128)} %bitcast.32), kind=kOutput, calls=%fused_computation.1 | convolution fusion | flops 905969664 | bytes 6488064 | tf_op jit(solution)/shard_map/dot_general | solution.py:15
  5.6 0.5 copy.5
  6.0 0.1 dynamic-slice_bitcast_fusion.1
  6.1 1.9 %collective-permute-start = (f32[16,96,128]{2,1,0:T(8,128)S(1)}, f32[16,96,128]{2,1,0:T(8,128)S(1)}, u32[]{:S(2)}, u32[]{:S(2)}) collective-permute-start(f32[16,96,128]{2,1,0:T(8,128)S(1)} %dynamic-slice_bitcast_fusion.1), channel_id=1, source_target_pairs={{0,1},{1,0},{2,3},{3,2},{4,5},{5,4},{6,7},{7,6},{8,9},{9,8},{10,11... | collective-permute-start | bytes 2359304 | tf_op jit(solution)/shard_map/ppermute | solution.py:29
  8.0 2.3 %collective-permute-done = f32[16,96,128]{2,1,0:T(8,128)S(1)} collective-permute-done((f32[16,96,128]{2,1,0:T(8,128)S(1)}, f32[16,96,128]{2,1,0:T(8,128)S(1)}, u32[]{:S(2)}, u32[]{:S(2)}) %collective-permute-start) | collective-permute-done | bytes 786464 | tf_op jit(solution)/shard_map/ppermute | solution.py:29
  10.3 0.1 bitcast_add_fusion.1
  10.4 0.0 copy-start
  10.4 21.6 %all_to_all.10 = f32[16,96,128]{2,1,0:T(8,128)S(1)} all-to-all(f32[16,96,128]{2,1,0:T(8,128)S(1)} %bitcast_add_fusion.1), channel_id=1, replica_groups=mesh['site'=16,'y'=4,'x'=4,'core'=2] {'y','x'}, dimensions={0} | all-to-all | bytes 1572864 | tf_op jit(solution)/shard_map/all_to_all | solution.py:30
  32.0 3.8 %collective-permute-start.1 = (f32[96,128]{1,0:T(8,128)S(1)}, f32[96,128]{1,0:T(8,128)S(1)}, u32[]{:S(2)}, u32[]{:S(2)}) collective-permute-start(f32[96,128]{1,0:T(8,128)S(1)} %reduce_sum.18), channel_id=1, source_target_pairs={{0,32},{32,64},{64,96},{96,128},{128,160},{160,192},{192,224},{224... | collective-permute-start | bytes 147464 | tf_op jit(solution)/shard_map/ppermute | solution.py:45
  35.9 3.3 %collective-permute-done.1 = f32[96,128]{1,0:T(8,128)S(1)} collective-permute-done((f32[96,128]{1,0:T(8,128)S(1)}, f32[96,128]{1,0:T(8,128)S(1)}, u32[]{:S(2)}, u32[]{:S(2)}) %collective-permute-start.1) | collective-permute-done | bytes 49184 | tf_op jit(solution)/shard_map/ppermute | solution.py:45
  39.2 0.0 copy-done
  39.3 4.0 %convolution_bitcast_fusion = f32[3072,128]{0,1:T(8,128)S(1)} fusion(f32[384,128]{1,0:T(8,128)S(1)} %bitcast.38, f32[384,3072]{1,0:T(8,128)} %bitcast.33), kind=kOutput, calls=%fused_computation | convolution fusion | flops 905969664 | bytes 6488064 | tf_op jit(solution)/shard_map/dot_general | solution.py:15
  43.2 0.5 copy.6
  43.7 0.1 dynamic-slice_bitcast_fusion
  43.8 1.9 %collective-permute-start.2 = (f32[16,96,128]{2,1,0:T(8,128)S(1)}, f32[16,96,128]{2,1,0:T(8,128)S(1)}, u32[]{:S(2)}, u32[]{:S(2)}) collective-permute-start(f32[16,96,128]{2,1,0:T(8,128)S(1)} %dynamic-slice_bitcast_fusion), channel_id=1, source_target_pairs={{0,1},{1,0},{2,3},{3,2},{4,5},{5,4},{6,7},{7,6},{8,9},{9,8},{10,11... | collective-permute-start | bytes 2359304 | tf_op jit(solution)/shard_map/ppermute | solution.py:29
  45.7 2.3 %collective-permute-done.2 = f32[16,96,128]{2,1,0:T(8,128)S(1)} collective-permute-done((f32[16,96,128]{2,1,0:T(8,128)S(1)}, f32[16,96,128]{2,1,0:T(8,128)S(1)}, u32[]{:S(2)}, u32[]{:S(2)}) %collective-permute-start.2) | collective-permute-done | bytes 786464 | tf_op jit(solution)/shard_map/ppermute | solution.py:29
  48.0 0.1 bitcast_add_fusion
  48.1 17.5 %all_to_all.11 = f32[16,96,128]{2,1,0:T(8,128)S(1)} all-to-all(f32[16,96,128]{2,1,0:T(8,128)S(1)} %bitcast_add_fusion), channel_id=1, replica_groups=mesh['site'=16,'y'=4,'x'=4,'core'=2] {'y','x'}, dimensions={0} | all-to-all | bytes 1572864 | tf_op jit(solution)/shard_map/all_to_all | solution.py:30
  65.6 0.6 maximum_bitcast_fusion
  (6 shorter events, 0.1 us)
Async XLA Ops:
  6.1 4.2 %collective-permute-start = (f32[16,96,128]{2,1,0:T(8,128)S(1)}, f32[16,96,128]{2,1,0:T(8,128)S(1)}, u32[]{:S(2)}, u32[]{:S(2)}) collective-permute-start(f32[16,96,128]{2,1,0:T(8,128)S(1)} %dynamic-slice_bitcast_fusion.1), channel_id=1, source_target_pairs={{0,1},{1,0},{2,3},{3,2},{4,5},{5,4},{6,7},{7,6},{8,9},{9,8},{10,11... | collective-permute-start | bytes 2359304 | tf_op jit(solution)/shard_map/ppermute | solution.py:29
  10.4 28.9 %copy-start = (f32[1,96,128]{2,1,0:T(8,128)S(1)}, f32[1,96,128]{2,1,0:T(8,128)}, u32[]{:S(2)}) copy-start(f32[1,96,128]{2,1,0:T(8,128)} %param.6) | copy-start | bytes 147460
  32.0 7.2 %collective-permute-start.1 = (f32[96,128]{1,0:T(8,128)S(1)}, f32[96,128]{1,0:T(8,128)S(1)}, u32[]{:S(2)}, u32[]{:S(2)}) collective-permute-start(f32[96,128]{1,0:T(8,128)S(1)} %reduce_sum.18), channel_id=1, source_target_pairs={{0,32},{32,64},{64,96},{96,128},{128,160},{160,192},{192,224},{224... | collective-permute-start | bytes 147464 | tf_op jit(solution)/shard_map/ppermute | solution.py:45
  43.8 4.2 %collective-permute-start.2 = (f32[16,96,128]{2,1,0:T(8,128)S(1)}, f32[16,96,128]{2,1,0:T(8,128)S(1)}, u32[]{:S(2)}, u32[]{:S(2)}) collective-permute-start(f32[16,96,128]{2,1,0:T(8,128)S(1)} %dynamic-slice_bitcast_fusion), channel_id=1, source_target_pairs={{0,1},{1,0},{2,3},{3,2},{4,5},{5,4},{6,7},{7,6},{8,9},{9,8},{10,11... | collective-permute-start | bytes 2359304 | tf_op jit(solution)/shard_map/ppermute | solution.py:29

commit v2 on v1

v2 whole, which is shorter than its diff:
```python
import functools

import jax
import jax.numpy as jnp
from jax import lax
from jax.experimental import pallas as pl
from jax.experimental.pallas import tpu as pltpu
from jax.sharding import Mesh, PartitionSpec as P

TICKS = 2
CHIPS = ("y", "x")
BOND = ("y", "x", "core")
PARAMS = pltpu.CompilerParams(vmem_limit_bytes=24 * 1024 * 1024)
VMEM = pl.BlockSpec(memory_space=pltpu.VMEM)
HBM = pl.BlockSpec(memory_space=pltpu.HBM)


def halves(value):
    upper = value.astype(jnp.bfloat16)
    return upper, (value - upper.astype(jnp.float32)).astype(jnp.bfloat16)


def left_operand(vectors, selected, outcome_count):
    masked = [jnp.where(selected == outcome, vectors, 0.0) for outcome in range(outcome_count)]
    upper, rest = halves(jnp.concatenate(masked, axis=0).T)
    return jnp.concatenate([upper, upper, rest], axis=1)


def place_product(left, upper, rest, first, rows, core, kept_ref, sent_ref):
    right = jnp.concatenate([upper, rest, upper], axis=0)
    product = jnp.dot(left, right, preferred_element_type=jnp.float32)
    chips = product.shape[1] // (2 * rows)
    blocks = product.T.reshape(chips, 2, rows, product.shape[0])
    kept_ref[first : first + chips] = jnp.where(core == 0, blocks[:, 0], blocks[:, 1])
    sent_ref[first : first + chips] = jnp.where(core == 0, blocks[:, 1], blocks[:, 0])


def first_kernel(
    selected_hbm, vectors_hbm, tensor_hbm,
    kept_ref, sent_ref, halves_ref, selected_ref,
    vectors_ref, tensor_ref, small_sem, tensor_sem,
):
    _, outcome_count, rows, columns = tensor_hbm.shape
    pieces = 2
    width = columns // pieces
    small = [
        pltpu.make_async_copy(selected_hbm, selected_ref, small_sem.at[0]),
        pltpu.make_async_copy(vectors_hbm, vectors_ref, small_sem.at[1]),
    ]
    large = []
    for piece in range(pieces):
        columns_of = pl.ds(piece * width, width)
        large.append(
            pltpu.make_async_copy(
                tensor_hbm.at[0, :, :, columns_of],
                tensor_ref.at[:, :, columns_of],
                tensor_sem.at[piece],
            )
        )
    for copy in small + large:
        copy.start()
    for copy in small:
        copy.wait()
    left = left_operand(vectors_ref[0], selected_ref[0, 0:1], outcome_count)
    for piece in range(pieces):
        large[piece].wait()
        span = slice(piece * width, (piece + 1) * width)
        upper, rest = halves(tensor_ref[:, :, span].reshape(outcome_count * rows, width))
        halves_ref[: outcome_count * rows, span] = upper
        halves_ref[outcome_count * rows :, span] = rest
        first = piece * width // (2 * rows)
        place_product(left, upper, rest, first, rows, lax.axis_index("core"), kept_ref, sent_ref)


def later_kernel(tick, selected_ref, fresh_ref, passed_ref, halves_ref, kept_ref, sent_ref):
    rows = passed_ref.shape[0]
    vectors = jnp.where(lax.axis_index("site") == 0, fresh_ref[tick - 1], passed_ref[...])
    stacked, columns = halves_ref.shape[0] // 2, halves_ref.shape[1]
    left = left_operand(vectors, selected_ref[0, tick : tick + 1], stacked // rows)
    pieces = 2
    width = columns // pieces
    for piece in range(pieces):
        span = slice(piece * width, (piece + 1) * width)
        first = piece * width // (2 * rows)
        upper, rest = halves_ref[:stacked, span], halves_ref[stacked:, span]
        place_product(left, upper, rest, first, rows, lax.axis_index("core"), kept_ref, sent_ref)


def cost(stacked, columns, samples, read):
    return pl.CostEstimate(
        flops=6 * stacked * columns * samples, bytes_accessed=read, transcendentals=0
    )


def first_product(outcomes, panels, site_tensor):
    _, outcome_count, rows, columns = site_tensor.shape
    samples = panels.shape[-1]
    stacked = outcome_count * rows
    block = pltpu.VMEM((columns // (2 * rows), rows, samples), jnp.float32)
    both = pltpu.VMEM((2 * stacked, columns), jnp.bfloat16)
    in_hbm = [pltpu.with_memory_space_constraint(a, pltpu.HBM) for a in (outcomes, panels, site_tensor)]
    return pl.pallas_call(
        first_kernel,
        out_shape=[block, block, both, pltpu.VMEM(outcomes.shape, outcomes.dtype)],
        in_specs=[HBM, HBM, HBM],
        out_specs=[VMEM] * 4,
        scratch_shapes=[
            pltpu.VMEM(panels.shape, panels.dtype),
            pltpu.VMEM((outcome_count, rows, columns), jnp.float32),
            pltpu.SemaphoreType.DMA((2,)),
            pltpu.SemaphoreType.DMA((2,)),
        ],
        compiler_params=PARAMS,
        cost_estimate=cost(stacked, columns, samples, 4 * stacked * columns),
        name="first_product",
    )(*in_hbm)


def later_product(tick, selected, fresh, passed, both):
    rows, samples = passed.shape
    stacked, columns = both.shape[0] // 2, both.shape[1]
    block = pltpu.VMEM((columns // (2 * rows), rows, samples), jnp.float32)
    return pl.pallas_call(
        functools.partial(later_kernel, tick),
        out_shape=[block, block],
        in_specs=[VMEM, VMEM, VMEM, VMEM],
        out_specs=[VMEM] * 2,
        compiler_params=PARAMS,
        cost_estimate=cost(stacked, columns, samples, 4 * columns * samples),
        name="later_product",
    )(selected, fresh, passed, both)


def scatter_sum(kept, sent):
    paired = kept + lax.ppermute(sent, "core", [(0, 1), (1, 0)])
    arrived = lax.all_to_all(paired, CHIPS, 0, 0, tiled=True)
    total = functools.reduce(jnp.add, [arrived[chip] for chip in range(arrived.shape[0])])
    return lax.optimization_barrier(total)


def on_device(site_tensor, panels, fresh, outcomes):
    sites = lax.axis_size("site")
    kept, sent, both, selected = first_product(outcomes, panels, site_tensor)
    results = [scatter_sum(kept, sent)]
    for tick in range(1, TICKS):
        passed = lax.ppermute(results[-1], "site", [(i, i + 1) for i in range(sites - 1)])
        results.append(scatter_sum(*later_product(tick, selected, fresh, passed, both)))
    return jnp.stack(results, 0)[None]


def solution(mesh):
    sites, bonds = mesh.devices.shape
    side = round((bonds // 2) ** 0.5)
    split = Mesh(mesh.devices.reshape(sites, side, side, 2), ("site", "y", "x", "core"))
    placed = (
        P("site", None, BOND, None),
        P("site", BOND, None),
        P(None, BOND, None),
        P("site", None, None),
    )
    return jax.shard_map(
        on_device,
        mesh=split,
        in_specs=placed,
        out_specs=P("site", None, BOND, None),
        check_vma=False,
    )
```

time: 66.7 us -> 60.7 us (0.910)
  matrix products: 7.93 us -> 0 us
  Pallas kernels: 0 us -> 4.92 us
  local copies, waits for them, and re-layouts: 1.81 us -> 0.01 us
  other arithmetic: 1.77 us -> 0.94 us
    dot_general x2 -> x0, matrix products: 7.93 us -> none  [contribute(): lax.dot_general(tensor.reshape(outcome_count * rows, columns), masked.res...]
    pallas_call x0 -> x2, Pallas kernels: none -> 4.92 us  [the longest x1 3.56 us: first_product(): pl.pallas_call(first_kernel, out_shape=[block, block, both, pltpu.VMEM(ou...]
    dot_general x2 -> x0, local copies, waits for them, and re-layouts: 0.92 us -> none  [contribute(): lax.dot_general(tensor.reshape(outcome_count * rows, columns), masked.res...]
    select_n x3 -> x0, other arithmetic: 0.84 us -> none  [the longest x2 0.83 us: contribute(): masked = jnp.where(chosen[:, None, :], vectors[None], 0.0)]
    eq x1 -> x0, local copies, waits for them, and re-layouts: 0.76 us -> none  [contribute(): selected[None, :] == jnp.arange(outcome_count, dtype=jnp.int32)[:, None]]
where the time goes in v2:
time: 60.7 us; the launch traced here: 60.5 us
  blocking collectives  39 us (64%)
  waiting for transfers between devices  7.86 us (13%)
  starting transfers between devices  7.67 us (13%)
  Pallas kernels  4.92 us (8%)
  other arithmetic  0.94 us (2%)
    all_to_all x2, blocking collectives, scatter_sum(): arrived = lax.all_to_all(paired, CHIPS, 0, 0, tiled=True)  39 us
    ppermute x2, waiting for transfers between devices, scatter_sum(): paired = kept + lax.ppermute(sent, 'core', [(0, 1), (1, 0)])  4.5 us
    ppermute x2, starting transfers between devices, scatter_sum(): paired = kept + lax.ppermute(sent, 'core', [(0, 1), (1, 0)])  3.84 us
    ppermute x1, starting transfers between devices, on_device(): lax.ppermute(results[-1], 'site', [(i, i + 1) for i in range(sites - 1)])  3.83 us
    pallas_call x1, Pallas kernels, first_product(): pl.pallas_call(first_kernel, out_shape=[block, block, both, pltpu.VMEM(ou...  3.56 us
    ppermute x1, waiting for transfers between devices, on_device(): lax.ppermute(results[-1], 'site', [(i, i + 1) for i in range(sites - 1)])  3.36 us
    pallas_call x1, Pallas kernels, later_product(): pl.pallas_call(functools.partial(later_kernel, tick), out_shape=[block, b...  1.36 us
  transfers between devices with their start and end apart: 3, of which 3 were waited for; matrix products, arithmetic and copies ran while one was open for 0% of the time, Pallas kernels for 0%

profile of v2, /device:TPU:128, one launch (start us, length us, event | category | flops | bytes accessed | tf_op | source)
XLA Modules:
  0.0 60.5 jit_solution(1724919233217642885)
XLA Ops:
  0.0 0.0 copy-start
  0.0 3.6 %first_product.1 = (f32[16,96,128]{2,1,0:T(8,128)S(1)}, f32[16,96,128]{2,1,0:T(8,128)S(1)}, bf16[768,3072]{1,0:T(8,128)(2,1)S(1)}, s32[1,2,128]{2,1,0:T(2,128)S(1)}) custom-call(s32[1,2,128]{2,1,0:T(2,128)} %selected_hbm.1, f32[1,96,128]{2,1,0:T(8,128)} %vectors_hbm.1, f32[1,4,96,3072]{3,2,1,0:T(8,128)} %tensor_hbm.1), custom_call_target="tpu_custom_call" | custom-call | flops 905969664 | bytes 4718592 | tf_op jit(solution)/shard_map/first_product/pallas_call | solution.py:102
  3.6 1.9 %collective-permute-start = (f32[16,96,128]{2,1,0:T(8,128)S(1)}, f32[16,96,128]{2,1,0:T(8,128)S(1)}, u32[]{:S(2)}, u32[]{:S(2)}) collective-permute-start(f32[16,96,128]{2,1,0:T(8,128)S(1)} %get-tuple-element.12), channel_id=1, source_target_pairs={{0,1},{1,0},{2,3},{3,2},{4,5},{5,4},{6,7},{7,6},{8,9},{9,8},{10,11... | collective-permute-start | bytes 2359304 | tf_op jit(solution)/shard_map/ppermute | solution.py:135
  5.5 2.3 %collective-permute-done = f32[16,96,128]{2,1,0:T(8,128)S(1)} collective-permute-done((f32[16,96,128]{2,1,0:T(8,128)S(1)}, f32[16,96,128]{2,1,0:T(8,128)S(1)}, u32[]{:S(2)}, u32[]{:S(2)}) %collective-permute-start) | collective-permute-done | bytes 786464 | tf_op jit(solution)/shard_map/ppermute | solution.py:135
  7.8 0.1 add.108
  7.8 21.5 %all_to_all.10 = f32[16,96,128]{2,1,0:T(8,128)S(1)} all-to-all(f32[16,96,128]{2,1,0:T(8,128)S(1)} %add.108), channel_id=1, replica_groups=mesh['site'=16,'y'=4,'x'=4,'core'=2] {'y','x'}, dimensions={0} | all-to-all | bytes 1572864 | tf_op jit(solution)/shard_map/all_to_all | solution.py:136
  29.4 3.8 %collective-permute-start.1 = (f32[96,128]{1,0:T(8,128)S(1)}, f32[96,128]{1,0:T(8,128)S(1)}, u32[]{:S(2)}, u32[]{:S(2)}) collective-permute-start(f32[96,128]{1,0:T(8,128)S(1)} %fusion.1), channel_id=1, source_target_pairs={{0,32},{32,64},{64,96},{96,128},{128,160},{160,192},{192,224},{224... | collective-permute-start | bytes 147464 | tf_op jit(solution)/shard_map/ppermute | solution.py:146
  33.2 3.4 %collective-permute-done.1.passed_ref = f32[96,128]{1,0:T(8,128)S(1)} collective-permute-done((f32[96,128]{1,0:T(8,128)S(1)}, f32[96,128]{1,0:T(8,128)S(1)}, u32[]{:S(2)}, u32[]{:S(2)}) %collective-permute-start.1) | collective-permute-done | bytes 49184 | tf_op jit(solution)/shard_map/ppermute | solution.py:146
  36.6 0.0 copy-done
  36.6 1.4 %later_product.1 = (f32[16,96,128]{2,1,0:T(8,128)S(1)}, f32[16,96,128]{2,1,0:T(8,128)S(1)}) custom-call(s32[1,2,128]{2,1,0:T(2,128)S(1)} %get-tuple-element.13.selected_ref, f32[1,96,128]{2,1,0:T(8,128)S(1)} %copy-done, f32[96,128]{1,0:T(8,128)S(1)} %collective-permute-done.1.passed_ref, bf16[768,3072]{1,0:T(8,128)(2,1)S(1)} %get-tuple-element.14.halves_ref), custom_call_target="tpu_custom_call" | custom-call | flops 905969664 | bytes 1572864 | tf_op jit(solution)/shard_map/later_product/pallas_call | solution.py:123
  37.9 1.9 %collective-permute-start.2 = (f32[16,96,128]{2,1,0:T(8,128)S(1)}, f32[16,96,128]{2,1,0:T(8,128)S(1)}, u32[]{:S(2)}, u32[]{:S(2)}) collective-permute-start(f32[16,96,128]{2,1,0:T(8,128)S(1)} %get-tuple-element.16), channel_id=1, source_target_pairs={{0,1},{1,0},{2,3},{3,2},{4,5},{5,4},{6,7},{7,6},{8,9},{9,8},{10,11... | collective-permute-start | bytes 2359304 | tf_op jit(solution)/shard_map/ppermute | solution.py:135
  39.9 2.3 %collective-permute-done.2 = f32[16,96,128]{2,1,0:T(8,128)S(1)} collective-permute-done((f32[16,96,128]{2,1,0:T(8,128)S(1)}, f32[16,96,128]{2,1,0:T(8,128)S(1)}, u32[]{:S(2)}, u32[]{:S(2)}) %collective-permute-start.2) | collective-permute-done | bytes 786464 | tf_op jit(solution)/shard_map/ppermute | solution.py:135
  42.1 0.1 add.125
  42.2 17.5 %all_to_all.11 = f32[16,96,128]{2,1,0:T(8,128)S(1)} all-to-all(f32[16,96,128]{2,1,0:T(8,128)S(1)} %add.125), channel_id=1, replica_groups=mesh['site'=16,'y'=4,'x'=4,'core'=2] {'y','x'}, dimensions={0} | all-to-all | bytes 1572864 | tf_op jit(solution)/shard_map/all_to_all | solution.py:136
  59.8 0.7 %maximum_bitcast_fusion = f32[1,2,96,128]{3,2,1,0:T(8,128)} fusion(f32[1,96,128]{2,1,0:T(8,128)S(1)} %bitcast.9, f32[1,96,128]{2,1,0:T(8,128)S(1)} %bitcast.8), kind=kLoop, calls=%fused_computation | loop fusion | flops 24576 | bytes 196608 | tf_op jit(solution)/shard_map/broadcast_in_dim | solution.py:148
  (2 shorter events, 0.1 us)
Async XLA Ops:
  0.0 36.6 %copy-start = (f32[1,96,128]{2,1,0:T(8,128)S(1)}, f32[1,96,128]{2,1,0:T(8,128)}, u32[]{:S(2)}) copy-start(f32[1,96,128]{2,1,0:T(8,128)} %fresh_ref.1) | copy-start | bytes 147460
  3.6 4.2 %collective-permute-start = (f32[16,96,128]{2,1,0:T(8,128)S(1)}, f32[16,96,128]{2,1,0:T(8,128)S(1)}, u32[]{:S(2)}, u32[]{:S(2)}) collective-permute-start(f32[16,96,128]{2,1,0:T(8,128)S(1)} %get-tuple-element.12), channel_id=1, source_target_pairs={{0,1},{1,0},{2,3},{3,2},{4,5},{5,4},{6,7},{7,6},{8,9},{9,8},{10,11... | collective-permute-start | bytes 2359304 | tf_op jit(solution)/shard_map/ppermute | solution.py:135
  29.4 7.2 %collective-permute-start.1 = (f32[96,128]{1,0:T(8,128)S(1)}, f32[96,128]{1,0:T(8,128)S(1)}, u32[]{:S(2)}, u32[]{:S(2)}) collective-permute-start(f32[96,128]{1,0:T(8,128)S(1)} %fusion.1), channel_id=1, source_target_pairs={{0,32},{32,64},{64,96},{96,128},{128,160},{160,192},{192,224},{224... | collective-permute-start | bytes 147464 | tf_op jit(solution)/shard_map/ppermute | solution.py:146
  37.9 4.2 %collective-permute-start.2 = (f32[16,96,128]{2,1,0:T(8,128)S(1)}, f32[16,96,128]{2,1,0:T(8,128)S(1)}, u32[]{:S(2)}, u32[]{:S(2)}) collective-permute-start(f32[16,96,128]{2,1,0:T(8,128)S(1)} %get-tuple-element.16), channel_id=1, source_target_pairs={{0,1},{1,0},{2,3},{3,2},{4,5},{5,4},{6,7},{7,6},{8,9},{9,8},{10,11... | collective-permute-start | bytes 2359304 | tf_op jit(solution)/shard_map/ppermute | solution.py:135

commit v3 on v2

v3 whole, which is shorter than its diff:
```python
import functools

import jax
import jax.numpy as jnp
from jax import lax
from jax.experimental import pallas as pl
from jax.experimental.pallas import tpu as pltpu
from jax.sharding import Mesh, PartitionSpec as P

TICKS = 2
CHIPS = ("y", "x")
BOND = ("y", "x", "core")
PARAMS = pltpu.CompilerParams(vmem_limit_bytes=24 * 1024 * 1024)
VMEM = pl.BlockSpec(memory_space=pltpu.VMEM)
HBM = pl.BlockSpec(memory_space=pltpu.HBM)


def halves(value):
    upper = value.astype(jnp.bfloat16)
    return upper, (value - upper.astype(jnp.float32)).astype(jnp.bfloat16)


def left_operand(vectors, selected, outcome_count):
    masked = [jnp.where(selected == outcome, vectors, 0.0) for outcome in range(outcome_count)]
    upper, rest = halves(jnp.concatenate(masked, axis=0).T)
    return jnp.concatenate([upper, upper, rest], axis=1)


def place_product(left, upper, rest, first, rows, core, kept_ref, sent_ref):
    right = jnp.concatenate([upper, rest, upper], axis=0)
    product = jnp.dot(left, right, preferred_element_type=jnp.float32)
    chips = product.shape[1] // (2 * rows)
    blocks = product.T.reshape(chips, 2, rows, product.shape[0])
    kept_ref[first : first + chips] = jnp.where(core == 0, blocks[:, 0], blocks[:, 1])
    sent_ref[first : first + chips] = jnp.where(core == 0, blocks[:, 1], blocks[:, 0])


def first_kernel(
    selected_hbm, vectors_hbm, fresh_hbm, tensor_hbm,
    kept_ref, sent_ref, tensor_ref, selected_ref,
    vectors_ref, small_sem, tensor_sem,
):
    _, outcome_count, rows, columns = tensor_hbm.shape
    pieces = 2
    width = columns // pieces
    small = [
        pltpu.make_async_copy(selected_hbm, selected_ref, small_sem.at[0]),
        pltpu.make_async_copy(vectors_hbm, vectors_ref, small_sem.at[1]),
        pltpu.make_async_copy(fresh_hbm, sent_ref.at[pl.ds(columns // (2 * rows), fresh_hbm.shape[0])], small_sem.at[2]),
    ]
    large = []
    for piece in range(pieces):
        columns_of = pl.ds(piece * width, width)
        large.append(
            pltpu.make_async_copy(
                tensor_hbm.at[0, :, :, columns_of],
                tensor_ref.at[:, :, columns_of],
                tensor_sem.at[piece],
            )
        )
    for copy in small + large:
        copy.start()
    for copy in small:
        copy.wait()
    left = left_operand(vectors_ref[0], selected_ref[0, 0:1], outcome_count)
    for piece in range(pieces):
        large[piece].wait()
        span = slice(piece * width, (piece + 1) * width)
        upper, rest = halves(tensor_ref[:, :, span].reshape(outcome_count * rows, width))
        first = piece * width // (2 * rows)
        place_product(left, upper, rest, first, rows, lax.axis_index("core"), kept_ref, sent_ref)


def split_kernel(tensor_ref, own_ref, other_ref):
    _, rows, columns = tensor_ref.shape
    own_first = lax.axis_index("core") == 0
    lane = lax.broadcasted_iota(jnp.int32, (rows, 128), 1)
    stacked = tensor_ref.shape[0] * rows
    for outcome in range(tensor_ref.shape[0]):
        band = slice(outcome * rows, (outcome + 1) * rows)
        low_band = slice(stacked + outcome * rows, stacked + (outcome + 1) * rows)
        for group in range(columns // 768):
            tile = [tensor_ref[outcome, :, group * 768 + 128 * i : group * 768 + 128 * (i + 1)] for i in range(6)]
            t0 = pltpu.roll(tile[0], 32, 1)
            t1 = pltpu.roll(tile[1], 32, 1)
            t2, t2b = pltpu.roll(tile[2], 32, 1), pltpu.roll(tile[2], 64, 1)
            t3, t3b = pltpu.roll(tile[3], 64, 1), pltpu.roll(tile[3], 96, 1)
            t4 = pltpu.roll(tile[4], 96, 1)
            t5 = pltpu.roll(tile[5], 96, 1)
            even = [
                jnp.where(lane < 96, tile[0], t1),
                jnp.where(lane < 32, t1, jnp.where(lane < 64, t2, t3)),
                jnp.where(lane < 32, t3, jnp.where(lane < 96, t4, t5)),
            ]
            odd = [
                jnp.where(lane < 32, t0, jnp.where(lane < 96, t1, t2b)),
                jnp.where(lane < 64, t2b, jnp.where(lane < 96, t3b, t4)),
                jnp.where(lane < 32, t4, tile[5]),
            ]
            for i in range(3):
                span = slice(group * 384 + 128 * i, group * 384 + 128 * (i + 1))
                upper, rest = halves(jnp.where(own_first, even[i], odd[i]))
                own_ref[band, span] = upper
                own_ref[low_band, span] = rest
                other_ref[band, span] = jnp.where(own_first, odd[i], even[i])


def later_kernel(
    tick, selected_ref, fresh_ref, received_ref, straight_ref, crossed_ref, own_ref, other_ref, paired_ref
):
    stacked, columns = other_ref.shape
    rows = straight_ref.shape[0]
    chips = columns // rows
    first = lax.axis_index("site") == 0
    selected = selected_ref[0, tick : tick + 1]
    mine = jnp.where(first, fresh_ref[tick - 1], straight_ref[...])
    theirs = jnp.where(first, received_ref[chips + tick - 1], crossed_ref[...])
    left = [left_operand(vectors, selected, stacked // rows) for vectors in (mine, theirs)]
    left = jnp.concatenate(left, axis=1)
    pieces = 2
    width = columns // pieces
    for piece in range(pieces):
        span = slice(piece * width, (piece + 1) * width)
        upper, rest = own_ref[:stacked, span], own_ref[stacked:, span]
        other_upper, other_rest = halves(other_ref[:, span])
        right = [upper, rest, upper, other_upper, other_rest, other_upper]
        product = jnp.dot(left, jnp.concatenate(right, axis=0), preferred_element_type=jnp.float32)
        blocks = product.T.reshape(chips // pieces, rows, product.shape[0])
        paired_ref[piece * chips // pieces : (piece + 1) * chips // pieces] = blocks


def cost(stacked, columns, samples, read):
    return pl.CostEstimate(
        flops=6 * stacked * columns * samples, bytes_accessed=read, transcendentals=0
    )


def first_product(outcomes, panels, fresh, site_tensor):
    _, outcome_count, rows, columns = site_tensor.shape
    samples = panels.shape[-1]
    stacked = outcome_count * rows
    chips = columns // (2 * rows)
    in_hbm = [
        pltpu.with_memory_space_constraint(a, pltpu.HBM)
        for a in (outcomes, panels, fresh, site_tensor)
    ]
    return pl.pallas_call(
        first_kernel,
        out_shape=[
            pltpu.VMEM((chips, rows, samples), jnp.float32),
            pltpu.VMEM((chips + fresh.shape[0], rows, samples), jnp.float32),
            pltpu.VMEM((outcome_count, rows, columns), jnp.float32),
            pltpu.VMEM(outcomes.shape, outcomes.dtype),
        ],
        in_specs=[HBM] * 4,
        out_specs=[VMEM] * 4,
        scratch_shapes=[
            pltpu.VMEM(panels.shape, panels.dtype),
            pltpu.SemaphoreType.DMA((3,)),
            pltpu.SemaphoreType.DMA((2,)),
        ],
        compiler_params=PARAMS,
        cost_estimate=cost(stacked, columns, samples, 4 * stacked * columns),
        name="first_product",
    )(*in_hbm)


def split_columns(tensor):
    outcome_count, rows, columns = tensor.shape
    stacked = outcome_count * rows
    return pl.pallas_call(
        split_kernel,
        out_shape=[
            pltpu.VMEM((2 * stacked, columns // 2), jnp.bfloat16),
            pltpu.VMEM((stacked, columns // 2), jnp.float32),
        ],
        in_specs=[VMEM],
        out_specs=[VMEM] * 2,
        compiler_params=PARAMS,
        cost_estimate=cost(stacked, columns, 128, 0),
        name="split_columns",
    )(tensor)


def later_product(tick, selected, fresh, received, straight, crossed, own, other):
    rows, samples = straight.shape
    stacked, columns = other.shape
    return pl.pallas_call(
        functools.partial(later_kernel, tick),
        out_shape=pltpu.VMEM((columns // rows, rows, samples), jnp.float32),
        in_specs=[VMEM] * 7,
        out_specs=VMEM,
        compiler_params=PARAMS,
        cost_estimate=cost(2 * stacked, columns, samples, 4 * columns * samples),
        name="later_product",
    )(selected, fresh, received, straight, crossed, own, other)


def pair_kernel(kept_ref, received_ref, paired_ref):
    paired_ref[...] = kept_ref[...] + received_ref[: kept_ref.shape[0]]


def pair_sum(kept, received):
    return pl.pallas_call(
        pair_kernel,
        out_shape=pltpu.VMEM(kept.shape, kept.dtype),
        in_specs=[VMEM] * 2,
        out_specs=VMEM,
        compiler_params=pltpu.CompilerParams(vmem_limit_bytes=4 * 1024 * 1024),
        cost_estimate=pl.CostEstimate(flops=10**11, bytes_accessed=10**8, transcendentals=0),
        name="pair_sum",
    )(kept, received)


def swapped(value):
    return lax.ppermute(value, "core", [(0, 1), (1, 0)])


def chip_sum(paired):
    arrived = lax.all_to_all(paired, CHIPS, 0, 0, tiled=True)
    total = functools.reduce(jnp.add, [arrived[chip] for chip in range(arrived.shape[0])])
    return lax.optimization_barrier(total)


def on_device(site_tensor, panels, fresh, outcomes):
    steps = [(i, i + 1) for i in range(lax.axis_size("site") - 1)]
    straight_pairs = [(2 * i + core, 2 * j + core) for i, j in steps for core in range(2)]
    crossed_pairs = [(2 * i + core, 2 * j + 1 - core) for i, j in steps for core in range(2)]
    kept, sent, tensor, selected = first_product(outcomes, panels, fresh, site_tensor)
    received = swapped(sent)
    own, other = split_columns(tensor)
    other = swapped(other)
    results = [chip_sum(pair_sum(kept, received))]
    for tick in range(1, TICKS):
        straight = lax.ppermute(results[-1], ("site", "core"), straight_pairs)
        crossed = lax.ppermute(results[-1], ("site", "core"), crossed_pairs)
        results.append(
            chip_sum(later_product(tick, selected, fresh, received, straight, crossed, own, other))
        )
    return jnp.stack(results, 0)[None]


def solution(mesh):
    sites, bonds = mesh.devices.shape
    side = round((bonds // 2) ** 0.5)
    split = Mesh(mesh.devices.reshape(sites, side, side, 2), ("site", "y", "x", "core"))
    placed = (
        P("site", None, BOND, None),
        P("site", BOND, None),
        P(None, BOND, None),
        P("site", None, None),
    )
    return jax.shard_map(
        on_device,
        mesh=split,
        in_specs=placed,
        out_specs=P("site", None, BOND, None),
        check_vma=False,
    )
```

time: 60.7 us -> 61.5 us (1.013)
  waiting for transfers between devices: 7.86 us -> 3.36 us
  starting transfers between devices: 7.67 us -> 10.5 us
  Pallas kernels: 4.92 us -> 6.79 us
  blocking collectives: 39 us -> 39.8 us
    ppermute x3 -> x4, waiting for transfers between devices: 7.86 us -> 3.36 us  [the longest x1 2.9 us: on_device(): straight = lax.ppermute(results[-1], ('site', 'core'), straight_pairs)]
    ppermute x3 -> x4, starting transfers between devices: 7.67 us -> 10.5 us  [the longest x2 4.33 us: swapped(): return lax.ppermute(value, 'core', [(0, 1), (1, 0)])]
    pallas_call x2 -> x4, Pallas kernels: 4.92 us -> 6.79 us  [the longest x1 3.52 us: first_product(): pl.pallas_call(first_kernel, out_shape=[pltpu.VMEM((chips, rows, samples)...]
    all_to_all x2, blocking collectives: 39 us -> 39.8 us  [chip_sum(): arrived = lax.all_to_all(paired, CHIPS, 0, 0, tiled=True)]
  transfers between devices with their start and end apart: 3 -> 4, of which waited for: 3 -> 2; matrix products, arithmetic and copies ran while one was open for 0% -> 0% of each run, Pallas kernels for 0% -> 3%
where the time goes in v3:
time: 61.5 us; the launch traced here: 61.2 us
  blocking collectives  39.8 us (65%)
  starting transfers between devices  10.5 us (17%)
  Pallas kernels  6.79 us (11%)
  waiting for transfers between devices  3.36 us (5%)
  other arithmetic  0.74 us (1%)
    all_to_all x2, blocking collectives, chip_sum(): arrived = lax.all_to_all(paired, CHIPS, 0, 0, tiled=True)  39.8 us
    ppermute x2, starting transfers between devices, swapped(): return lax.ppermute(value, 'core', [(0, 1), (1, 0)])  4.33 us
    ppermute x1, starting transfers between devices, on_device(): straight = lax.ppermute(results[-1], ('site', 'core'), straight_pairs)  3.83 us
    pallas_call x1, Pallas kernels, first_product(): pl.pallas_call(first_kernel, out_shape=[pltpu.VMEM((chips, rows, samples)...  3.52 us
    ppermute x1, waiting for transfers between devices, on_device(): straight = lax.ppermute(results[-1], ('site', 'core'), straight_pairs)  2.9 us
    ppermute x1, starting transfers between devices, on_device(): crossed = lax.ppermute(results[-1], ('site', 'core'), crossed_pairs)  2.32 us
    pallas_call x1, Pallas kernels, split_columns(): pl.pallas_call(split_kernel, out_shape=[pltpu.VMEM((2 * stacked, columns...  1.76 us
    pallas_call x1, Pallas kernels, later_product(): pl.pallas_call(functools.partial(later_kernel, tick), out_shape=pltpu.VME...  1.4 us
  transfers between devices with their start and end apart: 4, of which 2 were waited for; matrix products, arithmetic and copies ran while one was open for 0% of the time, Pallas kernels for 3%

profile of v3, /device:TPU:128, one launch (start us, length us, event | category | flops | bytes accessed | tf_op | source)
XLA Modules:
  0.0 61.2 jit_solution(5203733707614386792)
XLA Ops:
  0.0 3.5 %first_product.1 = (f32[16,96,128]{2,1,0:T(8,128)S(1)}, f32[17,96,128]{2,1,0:T(8,128)S(1)}, f32[4,96,3072]{2,1,0:T(8,128)S(1)}, s32[1,2,128]{2,1,0:T(2,128)S(1)}) custom-call(s32[1,2,128]{2,1,0:T(2,128)} %selected_hbm.1, f32[1,96,128]{2,1,0:T(8,128)} %vectors_hbm.1, f32[1,96,128]{2,1,0:T(8,128)} %fresh_ref.1, f32[1,4,96,3072]{3,2,1,0:T(8,128)} %tensor_hbm.1), custom_call_target="tpu_custom_call" | custom-call | flops 905969664 | bytes 4718592 | tf_op jit(solution)/shard_map/first_product/pallas_call | solution.py:147
  3.5 1.9 %collective-permute-start = (f32[17,96,128]{2,1,0:T(8,128)S(1)}, f32[17,96,128]{2,1,0:T(8,128)S(1)}, u32[]{:S(2)}, u32[]{:S(2)}) collective-permute-start(f32[17,96,128]{2,1,0:T(8,128)S(1)} %get-tuple-element.12), channel_id=1, source_target_pairs={{0,1},{1,0},{2,3},{3,2},{4,5},{5,4},{6,7},{7,6},{8,9},{9,8},{10,11... | collective-permute-start | bytes 2506760 | tf_op jit(solution)/shard_map/ppermute | solution.py:216
  5.5 1.8 %split_columns.1 = (bf16[768,1536]{1,0:T(8,128)(2,1)S(1)}, f32[384,1536]{1,0:T(8,128)S(1)}) custom-call(f32[4,96,3072]{2,1,0:T(8,128)S(1)} %get-tuple-element.14.tensor_ref), custom_call_target="tpu_custom_call" | custom-call | flops 905969664 | tf_op jit(solution)/shard_map/split_columns/pallas_call | solution.py:171
  7.2 2.4 %collective-permute-start.3 = (f32[384,1536]{1,0:T(8,128)S(1)}, f32[384,1536]{1,0:T(8,128)S(1)}, u32[]{:S(2)}, u32[]{:S(2)}) collective-permute-start(f32[384,1536]{1,0:T(8,128)S(1)} %get-tuple-element.16), channel_id=1, source_target_pairs={{0,1},{1,0},{2,3},{3,2},{4,5},{5,4},{6,7},{7,6},{8,9},{9,8},{10,11... | collective-permute-start | bytes 7077896 | tf_op jit(solution)/shard_map/ppermute | solution.py:216
  9.6 0.0 collective-permute-done.received_ref
  9.6 0.1 pair_sum.1
  9.8 0.0 copy-start
  9.8 21.5 %all_to_all.10 = f32[16,96,128]{2,1,0:T(8,128)S(1)} all-to-all(f32[16,96,128]{2,1,0:T(8,128)S(1)} %pair_sum.1), channel_id=1, replica_groups=mesh['site'=16,'y'=4,'x'=4,'core'=2] {'y','x'}, dimensions={0} | all-to-all | bytes 1572864 | tf_op jit(solution)/shard_map/all_to_all | solution.py:220
  31.3 2.3 %collective-permute-start.2 = (f32[96,128]{1,0:T(8,128)S(1)}, f32[96,128]{1,0:T(8,128)S(1)}, u32[]{:S(2)}, u32[]{:S(2)}) collective-permute-start(f32[96,128]{1,0:T(8,128)S(1)} %fusion.1), channel_id=1, source_target_pairs={{0,33},{1,32},{32,65},{33,64},{64,97},{65,96},{96,129},{97,128},{1... | collective-permute-start | bytes 147464 | tf_op jit(solution)/shard_map/ppermute | solution.py:236
  33.6 3.8 %collective-permute-start.1 = (f32[96,128]{1,0:T(8,128)S(1)}, f32[96,128]{1,0:T(8,128)S(1)}, u32[]{:S(2)}, u32[]{:S(2)}) collective-permute-start(f32[96,128]{1,0:T(8,128)S(1)} %fusion.1), channel_id=1, source_target_pairs={{0,32},{1,33},{32,64},{33,65},{64,96},{65,97},{96,128},{97,129},{1... | collective-permute-start | bytes 147464 | tf_op jit(solution)/shard_map/ppermute | solution.py:235
  37.5 0.5 collective-permute-done.2.crossed_ref
  37.9 2.9 %collective-permute-done.1.straight_ref = f32[96,128]{1,0:T(8,128)S(1)} collective-permute-done((f32[96,128]{1,0:T(8,128)S(1)}, f32[96,128]{1,0:T(8,128)S(1)}, u32[]{:S(2)}, u32[]{:S(2)}) %collective-permute-start.1) | collective-permute-done | bytes 49184 | tf_op jit(solution)/shard_map/ppermute | solution.py:235
  40.8 0.0 collective-permute-done.3.other_ref
  40.8 0.0 copy-done
  40.8 1.4 %later_product.1 = f32[16,96,128]{2,1,0:T(8,128)S(1)} custom-call(s32[1,2,128]{2,1,0:T(2,128)S(1)} %get-tuple-element.13.selected_ref, f32[1,96,128]{2,1,0:T(8,128)S(1)} %copy-done, f32[17,96,128]{2,1,0:T(8,128)S(1)} %collective-permute-done.received_ref, f32[96,128]{1,0:T(8,128)S(1)} %collective-permute-done.1.straight_ref, ...), custom_call_target="tpu_custom_call" | custom-call | flops 905969664 | bytes 786432 | tf_op jit(solution)/shard_map/later_product/pallas_call | solution.py:188
  42.2 18.3 %all_to_all.11 = f32[16,96,128]{2,1,0:T(8,128)S(1)} all-to-all(f32[16,96,128]{2,1,0:T(8,128)S(1)} %later_product.1), channel_id=1, replica_groups=mesh['site'=16,'y'=4,'x'=4,'core'=2] {'y','x'}, dimensions={0} | all-to-all | bytes 1572864 | tf_op jit(solution)/shard_map/all_to_all | solution.py:220
  60.5 0.7 %maximum_bitcast_fusion = f32[1,2,96,128]{3,2,1,0:T(8,128)} fusion(f32[1,96,128]{2,1,0:T(8,128)S(1)} %bitcast.9, f32[1,96,128]{2,1,0:T(8,128)S(1)} %bitcast.8), kind=kLoop, calls=%fused_computation | loop fusion | flops 24576 | bytes 196608 | tf_op jit(solution)/shard_map/broadcast_in_dim | solution.py:240
  (2 shorter events, 0.1 us)
Async XLA Ops:
  3.5 6.1 %collective-permute-start = (f32[17,96,128]{2,1,0:T(8,128)S(1)}, f32[17,96,128]{2,1,0:T(8,128)S(1)}, u32[]{:S(2)}, u32[]{:S(2)}) collective-permute-start(f32[17,96,128]{2,1,0:T(8,128)S(1)} %get-tuple-element.12), channel_id=1, source_target_pairs={{0,1},{1,0},{2,3},{3,2},{4,5},{5,4},{6,7},{7,6},{8,9},{9,8},{10,11... | collective-permute-start | bytes 2506760 | tf_op jit(solution)/shard_map/ppermute | solution.py:216
  7.2 33.6 %collective-permute-start.3 = (f32[384,1536]{1,0:T(8,128)S(1)}, f32[384,1536]{1,0:T(8,128)S(1)}, u32[]{:S(2)}, u32[]{:S(2)}) collective-permute-start(f32[384,1536]{1,0:T(8,128)S(1)} %get-tuple-element.16), channel_id=1, source_target_pairs={{0,1},{1,0},{2,3},{3,2},{4,5},{5,4},{6,7},{7,6},{8,9},{9,8},{10,11... | collective-permute-start | bytes 7077896 | tf_op jit(solution)/shard_map/ppermute | solution.py:216
  9.8 31.1 %copy-start = (f32[1,96,128]{2,1,0:T(8,128)S(1)}, f32[1,96,128]{2,1,0:T(8,128)}, u32[]{:S(2)}) copy-start(f32[1,96,128]{2,1,0:T(8,128)} %fresh_ref.1) | copy-start | bytes 147460
  31.3 6.6 %collective-permute-start.2 = (f32[96,128]{1,0:T(8,128)S(1)}, f32[96,128]{1,0:T(8,128)S(1)}, u32[]{:S(2)}, u32[]{:S(2)}) collective-permute-start(f32[96,128]{1,0:T(8,128)S(1)} %fusion.1), channel_id=1, source_target_pairs={{0,33},{1,32},{32,65},{33,64},{64,97},{65,96},{96,129},{97,128},{1... | collective-permute-start | bytes 147464 | tf_op jit(solution)/shard_map/ppermute | solution.py:236
  33.6 7.2 %collective-permute-start.1 = (f32[96,128]{1,0:T(8,128)S(1)}, f32[96,128]{1,0:T(8,128)S(1)}, u32[]{:S(2)}, u32[]{:S(2)}) collective-permute-start(f32[96,128]{1,0:T(8,128)S(1)} %fusion.1), channel_id=1, source_target_pairs={{0,32},{1,33},{32,64},{33,65},{64,96},{65,97},{96,128},{97,129},{1... | collective-permute-start | bytes 147464 | tf_op jit(solution)/shard_map/ppermute | solution.py:235

commit v4 on v3

--- a/solution.py
+++ b/solution.py
@@ -35,9 +35,28 @@
     sent_ref[first : first + chips] = jnp.where(core == 0, blocks[:, 1], blocks[:, 0])
 
 
+def alternate(tensor_ref, outcome, group, parity):
+    at = group * 768
+    tile = [tensor_ref[outcome, :, at + 128 * i : at + 128 * (i + 1)] for i in range(6)]
+    lane = lax.broadcasted_iota(jnp.int32, tile[0].shape, 1)
+    turned = (None, 32, 32, 64, 96, 96) if parity == 0 else (32, 32, 64, 96, 96, None)
+    t = [value if by is None else pltpu.roll(value, by, 1) for value, by in zip(tile, turned)]
+    if parity == 0:
+        return [
+            jnp.where(lane < 96, t[0], t[1]),
+            jnp.where(lane < 32, t[1], jnp.where(lane < 64, t[2], t[3])),
+            jnp.where(lane < 32, t[3], jnp.where(lane < 96, t[4], t[5])),
+        ]
+    return [
+        jnp.where(lane < 32, t[0], jnp.where(lane < 96, t[1], t[2])),
+        jnp.where(lane < 64, t[2], jnp.where(lane < 96, t[3], t[4])),
+        jnp.where(lane < 32, t[4], t[5]),
+    ]
+
+
 def first_kernel(
     selected_hbm, vectors_hbm, fresh_hbm, tensor_hbm,
-    kept_ref, sent_ref, tensor_ref, selected_ref,
+    kept_ref, sent_ref, tensor_ref, other_ref, selected_ref,
     vectors_ref, small_sem, tensor_sem,
 ):
     _, outcome_count, rows, columns = tensor_hbm.shape
@@ -69,40 +88,33 @@
         upper, rest = halves(tensor_ref[:, :, span].reshape(outcome_count * rows, width))
         first = piece * width // (2 * rows)
         place_product(left, upper, rest, first, rows, lax.axis_index("core"), kept_ref, sent_ref)
-
-
-def split_kernel(tensor_ref, own_ref, other_ref):
+        for parity in range(2):
+
+            @pl.when(lax.axis_index("core") == 1 - parity)
+            def _():
+                for outcome in range(outcome_count):
+                    for group in range(piece * width // 768, (piece + 1) * width // 768):
+                        for i, tile in enumerate(alternate(tensor_ref, outcome, group, parity)):
+                            begin = group * 384 + 128 * i
+                            other_ref[outcome * rows : (outcome + 1) * rows, begin : begin + 128] = tile
+
+
+def own_kernel(tensor_ref, own_ref):
     _, rows, columns = tensor_ref.shape
-    own_first = lax.axis_index("core") == 0
-    lane = lax.broadcasted_iota(jnp.int32, (rows, 128), 1)
     stacked = tensor_ref.shape[0] * rows
-    for outcome in range(tensor_ref.shape[0]):
-        band = slice(outcome * rows, (outcome + 1) * rows)
-        low_band = slice(stacked + outcome * rows, stacked + (outcome + 1) * rows)
-        for group in range(columns // 768):
-            tile = [tensor_ref[outcome, :, group * 768 + 128 * i : group * 768 + 128 * (i + 1)] for i in range(6)]
-            t0 = pltpu.roll(tile[0], 32, 1)
-            t1 = pltpu.roll(tile[1], 32, 1)
-            t2, t2b = pltpu.roll(tile[2], 32, 1), pltpu.roll(tile[2], 64, 1)
-            t3, t3b = pltpu.roll(tile[3], 64, 1), pltpu.roll(tile[3], 96, 1)
-            t4 = pltpu.roll(tile[4], 96, 1)
-            t5 = pltpu.roll(tile[5], 96, 1)
-            even = [
-                jnp.where(lane < 96, tile[0], t1),
-                jnp.where(lane < 32, t1, jnp.where(lane < 64, t2, t3)),
-                jnp.where(lane < 32, t3, jnp.where(lane < 96, t4, t5)),
-            ]
-            odd = [
-                jnp.where(lane < 32, t0, jnp.where(lane < 96, t1, t2b)),
-                jnp.where(lane < 64, t2b, jnp.where(lane < 96, t3b, t4)),
-                jnp.where(lane < 32, t4, tile[5]),
-            ]
-            for i in range(3):
-                span = slice(group * 384 + 128 * i, group * 384 + 128 * (i + 1))
-                upper, rest = halves(jnp.where(own_first, even[i], odd[i]))
-                own_ref[band, span] = upper
-                own_ref[low_band, span] = rest
-                other_ref[band, span] = jnp.where(own_first, odd[i], even[i])
+    core = lax.axis_index("core")
+    for parity in range(2):
+
+        @pl.when(core == parity)
+        def _():
+            for outcome in range(tensor_ref.shape[0]):
+                for group in range(columns // 768):
+                    for i, tile in enumerate(alternate(tensor_ref, outcome, group, parity)):
+                        span = slice(group * 384 + 128 * i, group * 384 + 128 * (i + 1))
+                        first = outcome * rows
+                        upper, rest = halves(tile)
+                        own_ref[first : first + rows, span] = upper
+                        own_ref[stacked + first : stacked + first + rows, span] = rest
 
 
 def later_kernel(
@@ -150,10 +162,11 @@
             pltpu.VMEM((chips, rows, samples), jnp.float32),
             pltpu.VMEM((chips + fresh.shape[0], rows, samples), jnp.float32),
             pltpu.VMEM((outcome_count, rows, columns), jnp.float32),
+            pltpu.VMEM((stacked, columns // 2), jnp.float32),
             pltpu.VMEM(outcomes.shape, outcomes.dtype),
         ],
         in_specs=[HBM] * 4,
-        out_specs=[VMEM] * 4,
+        out_specs=[VMEM] * 5,
         scratch_shapes=[
             pltpu.VMEM(panels.shape, panels.dtype),
             pltpu.SemaphoreType.DMA((3,)),
@@ -165,20 +178,17 @@
     )(*in_hbm)
 
 
-def split_columns(tensor):
+def own_columns(tensor):
     outcome_count, rows, columns = tensor.shape
     stacked = outcome_count * rows
     return pl.pallas_call(
-        split_kernel,
-        out_shape=[
-            pltpu.VMEM((2 * stacked, columns // 2), jnp.bfloat16),
-            pltpu.VMEM((stacked, columns // 2), jnp.float32),
-        ],
+        own_kernel,
+        out_shape=pltpu.VMEM((2 * stacked, columns // 2), jnp.bfloat16),
         in_specs=[VMEM],
-        out_specs=[VMEM] * 2,
+        out_specs=VMEM,
         compiler_params=PARAMS,
-        cost_estimate=cost(stacked, columns, 128, 0),
-        name="split_columns",
+        cost_estimate=cost(stacked, columns, 256, 0),
+        name="own_columns",
     )(tensor)
 
 
@@ -226,14 +236,14 @@
     steps = [(i, i + 1) for i in range(lax.axis_size("site") - 1)]
     straight_pairs = [(2 * i + core, 2 * j + core) for i, j in steps for core in range(2)]
     crossed_pairs = [(2 * i + core, 2 * j + 1 - core) for i, j in steps for core in range(2)]
-    kept, sent, tensor, selected = first_product(outcomes, panels, fresh, site_tensor)
+    kept, sent, tensor, other, selected = first_product(outcomes, panels, fresh, site_tensor)
     received = swapped(sent)
-    own, other = split_columns(tensor)
     other = swapped(other)
     results = [chip_sum(pair_sum(kept, received))]
     for tick in range(1, TICKS):
         straight = lax.ppermute(results[-1], ("site", "core"), straight_pairs)
         crossed = lax.ppermute(results[-1], ("site", "core"), crossed_pairs)
+        own = own_columns(tensor)
         results.append(
             chip_sum(later_product(tick, selected, fresh, received, straight, crossed, own, other))
         )

time: 61.5 us -> 61 us (level)
  the two profiles are of different devices: /device:TPU:128 before, /device:TPU:224 now
where the time goes in v4:
time: 61 us; the launch traced here: 60.7 us
  blocking collectives  39.9 us (65%)
  starting transfers between devices  11.3 us (19%)
  Pallas kernels  7.26 us (12%)
  waiting for transfers between devices  1.45 us (2%)
  other arithmetic  0.74 us (1%)
    all_to_all x2, blocking collectives, chip_sum(): arrived = lax.all_to_all(paired, CHIPS, 0, 0, tiled=True)  39.9 us
    pallas_call x1, Pallas kernels, first_product(): pl.pallas_call(first_kernel, out_shape=[pltpu.VMEM((chips, rows, samples)...  4.65 us
    ppermute x2, starting transfers between devices, swapped(): return lax.ppermute(value, 'core', [(0, 1), (1, 0)])  4.33 us
    ppermute x1, starting transfers between devices, on_device(): crossed = lax.ppermute(results[-1], ('site', 'core'), crossed_pairs)  3.54 us
    ppermute x1, starting transfers between devices, on_device(): straight = lax.ppermute(results[-1], ('site', 'core'), straight_pairs)  3.41 us
    ppermute x1, waiting for transfers between devices, on_device(): straight = lax.ppermute(results[-1], ('site', 'core'), straight_pairs)  1.44 us
    pallas_call x1, Pallas kernels, later_product(): pl.pallas_call(functools.partial(later_kernel, tick), out_shape=pltpu.VME...  1.4 us
  transfers between devices with their start and end apart: 4, of which 1 were waited for; matrix products, arithmetic and copies ran while one was open for 0% of the time, Pallas kernels for 2%

profile of v4, /device:TPU:224, one launch (start us, length us, event | category | flops | bytes accessed | tf_op | source)
XLA Modules:
  0.0 60.7 jit_solution(6279256669714543395)
XLA Ops:
  0.0 4.7 %first_product.1 = (f32[16,96,128]{2,1,0:T(8,128)S(1)}, f32[17,96,128]{2,1,0:T(8,128)S(1)}, f32[4,96,3072]{2,1,0:T(8,128)S(1)}, f32[384,1536]{1,0:T(8,128)S(1)}, s32[1,2,128]{2,1,0:T(2,128)S(1)}) custom-call(s32[1,2,128]{2,1,0:T(2,128)} %selected_hbm.1, f32[1,96,128]{2,1,0:T(8,128)} %vectors_hbm.1, f32[1,96,128]{2,1,0:T(8,128)} %fresh_ref.1, ...), custom_call_target="tpu_custom_call" | custom-call | flops 905969664 | bytes 4718592 | tf_op jit(solution)/shard_map/first_product/pallas_call | solution.py:159
  4.7 1.9 %collective-permute-start = (f32[17,96,128]{2,1,0:T(8,128)S(1)}, f32[17,96,128]{2,1,0:T(8,128)S(1)}, u32[]{:S(2)}, u32[]{:S(2)}) collective-permute-start(f32[17,96,128]{2,1,0:T(8,128)S(1)} %get-tuple-element.11), channel_id=1, source_target_pairs={{0,1},{1,0},{2,3},{3,2},{4,5},{5,4},{6,7},{7,6},{8,9},{9,8},{10,11... | collective-permute-start | bytes 2506760 | tf_op jit(solution)/shard_map/ppermute | solution.py:226
  6.6 2.4 %collective-permute-start.3 = (f32[384,1536]{1,0:T(8,128)S(1)}, f32[384,1536]{1,0:T(8,128)S(1)}, u32[]{:S(2)}, u32[]{:S(2)}) collective-permute-start(f32[384,1536]{1,0:T(8,128)S(1)} %get-tuple-element.14), channel_id=1, source_target_pairs={{0,1},{1,0},{2,3},{3,2},{4,5},{5,4},{6,7},{7,6},{8,9},{9,8},{10,11... | collective-permute-start | bytes 7077896 | tf_op jit(solution)/shard_map/ppermute | solution.py:226
  9.0 0.0 collective-permute-done.received_ref
  9.0 0.1 pair_sum.1
  9.1 21.4 %all_to_all.10 = f32[16,96,128]{2,1,0:T(8,128)S(1)} all-to-all(f32[16,96,128]{2,1,0:T(8,128)S(1)} %pair_sum.1), channel_id=1, replica_groups=mesh['site'=16,'y'=4,'x'=4,'core'=2] {'y','x'}, dimensions={0} | all-to-all | bytes 1572864 | tf_op jit(solution)/shard_map/all_to_all | solution.py:230
  30.6 3.5 %collective-permute-start.2 = (f32[96,128]{1,0:T(8,128)S(1)}, f32[96,128]{1,0:T(8,128)S(1)}, u32[]{:S(2)}, u32[]{:S(2)}) collective-permute-start(f32[96,128]{1,0:T(8,128)S(1)} %fusion.1), channel_id=1, source_target_pairs={{0,33},{1,32},{32,65},{33,64},{64,97},{65,96},{96,129},{97,128},{1... | collective-permute-start | bytes 147464 | tf_op jit(solution)/shard_map/ppermute | solution.py:245
  34.1 3.4 %collective-permute-start.1 = (f32[96,128]{1,0:T(8,128)S(1)}, f32[96,128]{1,0:T(8,128)S(1)}, u32[]{:S(2)}, u32[]{:S(2)}) collective-permute-start(f32[96,128]{1,0:T(8,128)S(1)} %fusion.1), channel_id=1, source_target_pairs={{0,32},{1,33},{32,64},{33,65},{64,96},{65,97},{96,128},{97,129},{1... | collective-permute-start | bytes 147464 | tf_op jit(solution)/shard_map/ppermute | solution.py:244
  37.5 0.0 copy-start
  37.5 1.1 %own_columns.1.own_ref = bf16[768,1536]{1,0:T(8,128)(2,1)S(1)} custom-call(f32[4,96,3072]{2,1,0:T(8,128)S(1)} %get-tuple-element.13.tensor_ref), custom_call_target="tpu_custom_call" | custom-call | flops 1811939328 | tf_op jit(solution)/shard_map/own_columns/pallas_call | solution.py:184
  38.6 0.0 collective-permute-done.2.crossed_ref
  38.7 1.4 %collective-permute-done.1.straight_ref = f32[96,128]{1,0:T(8,128)S(1)} collective-permute-done((f32[96,128]{1,0:T(8,128)S(1)}, f32[96,128]{1,0:T(8,128)S(1)}, u32[]{:S(2)}, u32[]{:S(2)}) %collective-permute-start.1) | collective-permute-done | bytes 49184 | tf_op jit(solution)/shard_map/ppermute | solution.py:244
  40.1 0.0 collective-permute-done.3.other_ref
  40.1 0.0 copy-done
  40.1 1.4 %later_product.1 = f32[16,96,128]{2,1,0:T(8,128)S(1)} custom-call(s32[1,2,128]{2,1,0:T(2,128)S(1)} %get-tuple-element.12.selected_ref, f32[1,96,128]{2,1,0:T(8,128)S(1)} %copy-done, f32[17,96,128]{2,1,0:T(8,128)S(1)} %collective-permute-done.received_ref, f32[96,128]{1,0:T(8,128)S(1)} %collective-permute-done.1.straight_ref, ...), custom_call_target="tpu_custom_call" | custom-call | flops 905969664 | bytes 786432 | tf_op jit(solution)/shard_map/later_product/pallas_call | solution.py:198
  41.5 18.5 %all_to_all.11 = f32[16,96,128]{2,1,0:T(8,128)S(1)} all-to-all(f32[16,96,128]{2,1,0:T(8,128)S(1)} %later_product.1), channel_id=1, replica_groups=mesh['site'=16,'y'=4,'x'=4,'core'=2] {'y','x'}, dimensions={0} | all-to-all | bytes 1572864 | tf_op jit(solution)/shard_map/all_to_all | solution.py:230
  60.1 0.6 %maximum_bitcast_fusion = f32[1,2,96,128]{3,2,1,0:T(8,128)} fusion(f32[1,96,128]{2,1,0:T(8,128)S(1)} %bitcast.9, f32[1,96,128]{2,1,0:T(8,128)S(1)} %bitcast.8), kind=kLoop, calls=%fused_computation | loop fusion | flops 24576 | bytes 196608 | tf_op jit(solution)/shard_map/broadcast_in_dim | solution.py:250
  (2 shorter events, 0.1 us)
Async XLA Ops:
  4.7 4.3 %collective-permute-start = (f32[17,96,128]{2,1,0:T(8,128)S(1)}, f32[17,96,128]{2,1,0:T(8,128)S(1)}, u32[]{:S(2)}, u32[]{:S(2)}) collective-permute-start(f32[17,96,128]{2,1,0:T(8,128)S(1)} %get-tuple-element.11), channel_id=1, source_target_pairs={{0,1},{1,0},{2,3},{3,2},{4,5},{5,4},{6,7},{7,6},{8,9},{9,8},{10,11... | collective-permute-start | bytes 2506760 | tf_op jit(solution)/shard_map/ppermute | solution.py:226
  6.6 33.5 %collective-permute-start.3 = (f32[384,1536]{1,0:T(8,128)S(1)}, f32[384,1536]{1,0:T(8,128)S(1)}, u32[]{:S(2)}, u32[]{:S(2)}) collective-permute-start(f32[384,1536]{1,0:T(8,128)S(1)} %get-tuple-element.14), channel_id=1, source_target_pairs={{0,1},{1,0},{2,3},{3,2},{4,5},{5,4},{6,7},{7,6},{8,9},{9,8},{10,11... | collective-permute-start | bytes 7077896 | tf_op jit(solution)/shard_map/ppermute | solution.py:226
  30.6 8.1 %collective-permute-start.2 = (f32[96,128]{1,0:T(8,128)S(1)}, f32[96,128]{1,0:T(8,128)S(1)}, u32[]{:S(2)}, u32[]{:S(2)}) collective-permute-start(f32[96,128]{1,0:T(8,128)S(1)} %fusion.1), channel_id=1, source_target_pairs={{0,33},{1,32},{32,65},{33,64},{64,97},{65,96},{96,129},{97,128},{1... | collective-permute-start | bytes 147464 | tf_op jit(solution)/shard_map/ppermute | solution.py:245
  34.1 6.0 %collective-permute-start.1 = (f32[96,128]{1,0:T(8,128)S(1)}, f32[96,128]{1,0:T(8,128)S(1)}, u32[]{:S(2)}, u32[]{:S(2)}) collective-permute-start(f32[96,128]{1,0:T(8,128)S(1)} %fusion.1), channel_id=1, source_target_pairs={{0,32},{1,33},{32,64},{33,65},{64,96},{65,97},{96,128},{97,129},{1... | collective-permute-start | bytes 147464 | tf_op jit(solution)/shard_map/ppermute | solution.py:244
  37.5 2.6 %copy-start = (f32[1,96,128]{2,1,0:T(8,128)S(1)}, f32[1,96,128]{2,1,0:T(8,128)}, u32[]{:S(2)}) copy-start(f32[1,96,128]{2,1,0:T(8,128)} %fresh_ref.1) | copy-start | bytes 147460

commit v5 on v2

--- a/solution.py
+++ b/solution.py
@@ -37,8 +37,8 @@
 
 def first_kernel(
     selected_hbm, vectors_hbm, tensor_hbm,
-    kept_ref, sent_ref, halves_ref, selected_ref,
-    vectors_ref, tensor_ref, small_sem, tensor_sem,
+    kept_ref, sent_ref, tensor_ref, selected_ref,
+    vectors_ref, small_sem, tensor_sem,
 ):
     _, outcome_count, rows, columns = tensor_hbm.shape
     pieces = 2
@@ -66,10 +66,18 @@
         large[piece].wait()
         span = slice(piece * width, (piece + 1) * width)
         upper, rest = halves(tensor_ref[:, :, span].reshape(outcome_count * rows, width))
-        halves_ref[: outcome_count * rows, span] = upper
-        halves_ref[outcome_count * rows :, span] = rest
         first = piece * width // (2 * rows)
         place_product(left, upper, rest, first, rows, lax.axis_index("core"), kept_ref, sent_ref)
+
+
+def halves_kernel(tensor_ref, halves_ref):
+    outcome_count, rows, _ = tensor_ref.shape
+    stacked = outcome_count * rows
+    for outcome in range(outcome_count):
+        first = outcome * rows
+        upper, rest = halves(tensor_ref[outcome])
+        halves_ref[first : first + rows] = upper
+        halves_ref[stacked + first : stacked + first + rows] = rest
 
 
 def later_kernel(tick, selected_ref, fresh_ref, passed_ref, halves_ref, kept_ref, sent_ref):
@@ -97,16 +105,15 @@
     samples = panels.shape[-1]
     stacked = outcome_count * rows
     block = pltpu.VMEM((columns // (2 * rows), rows, samples), jnp.float32)
-    both = pltpu.VMEM((2 * stacked, columns), jnp.bfloat16)
+    whole = pltpu.VMEM((outcome_count, rows, columns), jnp.float32)
     in_hbm = [pltpu.with_memory_space_constraint(a, pltpu.HBM) for a in (outcomes, panels, site_tensor)]
     return pl.pallas_call(
         first_kernel,
-        out_shape=[block, block, both, pltpu.VMEM(outcomes.shape, outcomes.dtype)],
+        out_shape=[block, block, whole, pltpu.VMEM(outcomes.shape, outcomes.dtype)],
         in_specs=[HBM, HBM, HBM],
         out_specs=[VMEM] * 4,
         scratch_shapes=[
             pltpu.VMEM(panels.shape, panels.dtype),
-            pltpu.VMEM((outcome_count, rows, columns), jnp.float32),
             pltpu.SemaphoreType.DMA((2,)),
             pltpu.SemaphoreType.DMA((2,)),
         ],
@@ -114,6 +121,19 @@
         cost_estimate=cost(stacked, columns, samples, 4 * stacked * columns),
         name="first_product",
     )(*in_hbm)
+
+
+def tensor_halves(tensor):
+    outcome_count, rows, columns = tensor.shape
+    return pl.pallas_call(
+        halves_kernel,
+        out_shape=pltpu.VMEM((2 * outcome_count * rows, columns), jnp.bfloat16),
+        in_specs=[VMEM],
+        out_specs=VMEM,
+        compiler_params=PARAMS,
+        cost_estimate=cost(outcome_count * rows, columns, 128, 0),
+        name="tensor_halves",
+    )(tensor)
 
 
 def later_product(tick, selected, fresh, passed, both):
@@ -140,10 +160,11 @@
 
 def on_device(site_tensor, panels, fresh, outcomes):
     sites = lax.axis_size("site")
-    kept, sent, both, selected = first_product(outcomes, panels, site_tensor)
+    kept, sent, tensor, selected = first_product(outcomes, panels, site_tensor)
     results = [scatter_sum(kept, sent)]
     for tick in range(1, TICKS):
         passed = lax.ppermute(results[-1], "site", [(i, i + 1) for i in range(sites - 1)])
+        both = tensor_halves(tensor)
         results.append(scatter_sum(*later_product(tick, selected, fresh, passed, both)))
     return jnp.stack(results, 0)[None]
 

time: 60.7 us -> 60.7 us (level)
  the two profiles are of different devices: /device:TPU:128 before, /device:TPU:384 now
where the time goes in v5:
time: 60.7 us; the launch traced here: 60.4 us
  blocking collectives  39 us (64%)
  waiting for transfers between devices  8.07 us (13%)
  starting transfers between devices  6.79 us (11%)
  Pallas kernels  5.49 us (9%)
  other arithmetic  0.93 us (2%)
    all_to_all x2, blocking collectives, scatter_sum(): arrived = lax.all_to_all(paired, CHIPS, 0, 0, tiled=True)  39 us
    ppermute x2, waiting for transfers between devices, scatter_sum(): paired = kept + lax.ppermute(sent, 'core', [(0, 1), (1, 0)])  4.5 us
    ppermute x2, starting transfers between devices, scatter_sum(): paired = kept + lax.ppermute(sent, 'core', [(0, 1), (1, 0)])  3.84 us
    ppermute x1, waiting for transfers between devices, on_device(): lax.ppermute(results[-1], 'site', [(i, i + 1) for i in range(sites - 1)])  3.57 us
    pallas_call x1, Pallas kernels, first_product(): pl.pallas_call(first_kernel, out_shape=[block, block, whole, pltpu.VMEM(o...  3.48 us
    ppermute x1, starting transfers between devices, on_device(): lax.ppermute(results[-1], 'site', [(i, i + 1) for i in range(sites - 1)])  2.95 us
    pallas_call x1, Pallas kernels, later_product(): pl.pallas_call(functools.partial(later_kernel, tick), out_shape=[block, b...  1.36 us
  transfers between devices with their start and end apart: 3, of which 3 were waited for; matrix products, arithmetic and copies ran while one was open for 0% of the time, Pallas kernels for 1%

profile of v5, /device:TPU:384, one launch (start us, length us, event | category | flops | bytes accessed | tf_op | source)
XLA Modules:
  0.0 60.4 jit_solution(13261926448905857943)
XLA Ops:
  0.0 3.5 %first_product.1 = (f32[16,96,128]{2,1,0:T(8,128)S(1)}, f32[16,96,128]{2,1,0:T(8,128)S(1)}, f32[4,96,3072]{2,1,0:T(8,128)S(1)}, s32[1,2,128]{2,1,0:T(2,128)S(1)}) custom-call(s32[1,2,128]{2,1,0:T(2,128)} %selected_hbm.1, f32[1,96,128]{2,1,0:T(8,128)} %vectors_hbm.1, f32[1,4,96,3072]{3,2,1,0:T(8,128)} %tensor_hbm.1), custom_call_target="tpu_custom_call" | custom-call | flops 905969664 | bytes 4718592 | tf_op jit(solution)/shard_map/first_product/pallas_call | solution.py:110
  3.5 1.9 %collective-permute-start = (f32[16,96,128]{2,1,0:T(8,128)S(1)}, f32[16,96,128]{2,1,0:T(8,128)S(1)}, u32[]{:S(2)}, u32[]{:S(2)}) collective-permute-start(f32[16,96,128]{2,1,0:T(8,128)S(1)} %get-tuple-element.12), channel_id=1, source_target_pairs={{0,1},{1,0},{2,3},{3,2},{4,5},{5,4},{6,7},{7,6},{8,9},{9,8},{10,11... | collective-permute-start | bytes 2359304 | tf_op jit(solution)/shard_map/ppermute | solution.py:155
  5.4 2.3 %collective-permute-done = f32[16,96,128]{2,1,0:T(8,128)S(1)} collective-permute-done((f32[16,96,128]{2,1,0:T(8,128)S(1)}, f32[16,96,128]{2,1,0:T(8,128)S(1)}, u32[]{:S(2)}, u32[]{:S(2)}) %collective-permute-start) | collective-permute-done | bytes 786464 | tf_op jit(solution)/shard_map/ppermute | solution.py:155
  7.7 0.1 add.108
  7.8 21.5 %all_to_all.10 = f32[16,96,128]{2,1,0:T(8,128)S(1)} all-to-all(f32[16,96,128]{2,1,0:T(8,128)S(1)} %add.108), channel_id=1, replica_groups=mesh['site'=16,'y'=4,'x'=4,'core'=2] {'y','x'}, dimensions={0} | all-to-all | bytes 1572864 | tf_op jit(solution)/shard_map/all_to_all | solution.py:156
  29.3 2.9 %collective-permute-start.1 = (f32[96,128]{1,0:T(8,128)S(1)}, f32[96,128]{1,0:T(8,128)S(1)}, u32[]{:S(2)}, u32[]{:S(2)}) collective-permute-start(f32[96,128]{1,0:T(8,128)S(1)} %fusion.1), channel_id=1, source_target_pairs={{0,32},{32,64},{64,96},{96,128},{128,160},{160,192},{192,224},{224... | collective-permute-start | bytes 147464 | tf_op jit(solution)/shard_map/ppermute | solution.py:166
  32.2 0.0 copy-start
  32.2 0.7 %tensor_halves.1.halves_ref = bf16[768,3072]{1,0:T(8,128)(2,1)S(1)} custom-call(f32[4,96,3072]{2,1,0:T(8,128)S(1)} %get-tuple-element.14.tensor_ref), custom_call_target="tpu_custom_call" | custom-call | flops 905969664 | tf_op jit(solution)/shard_map/tensor_halves/pallas_call | solution.py:128
  32.9 3.6 %collective-permute-done.1.passed_ref = f32[96,128]{1,0:T(8,128)S(1)} collective-permute-done((f32[96,128]{1,0:T(8,128)S(1)}, f32[96,128]{1,0:T(8,128)S(1)}, u32[]{:S(2)}, u32[]{:S(2)}) %collective-permute-start.1) | collective-permute-done | bytes 49184 | tf_op jit(solution)/shard_map/ppermute | solution.py:166
  36.5 0.0 copy-done
  36.5 1.4 %later_product.1 = (f32[16,96,128]{2,1,0:T(8,128)S(1)}, f32[16,96,128]{2,1,0:T(8,128)S(1)}) custom-call(s32[1,2,128]{2,1,0:T(2,128)S(1)} %get-tuple-element.13.selected_ref, f32[1,96,128]{2,1,0:T(8,128)S(1)} %copy-done, f32[96,128]{1,0:T(8,128)S(1)} %collective-permute-done.1.passed_ref, bf16[768,3072]{1,0:T(8,128)(2,1)S(1)} %tensor_halves.1.halves_ref), custom_call_target="tpu_custom_call" | custom-call | flops 905969664 | bytes 1572864 | tf_op jit(solution)/shard_map/later_product/pallas_call | solution.py:143
  37.8 1.9 %collective-permute-start.2 = (f32[16,96,128]{2,1,0:T(8,128)S(1)}, f32[16,96,128]{2,1,0:T(8,128)S(1)}, u32[]{:S(2)}, u32[]{:S(2)}) collective-permute-start(f32[16,96,128]{2,1,0:T(8,128)S(1)} %get-tuple-element.16), channel_id=1, source_target_pairs={{0,1},{1,0},{2,3},{3,2},{4,5},{5,4},{6,7},{7,6},{8,9},{9,8},{10,11... | collective-permute-start | bytes 2359304 | tf_op jit(solution)/shard_map/ppermute | solution.py:155
  39.8 2.3 %collective-permute-done.2 = f32[16,96,128]{2,1,0:T(8,128)S(1)} collective-permute-done((f32[16,96,128]{2,1,0:T(8,128)S(1)}, f32[16,96,128]{2,1,0:T(8,128)S(1)}, u32[]{:S(2)}, u32[]{:S(2)}) %collective-permute-start.2) | collective-permute-done | bytes 786464 | tf_op jit(solution)/shard_map/ppermute | solution.py:155
  42.0 0.1 add.125
  42.1 17.5 %all_to_all.11 = f32[16,96,128]{2,1,0:T(8,128)S(1)} all-to-all(f32[16,96,128]{2,1,0:T(8,128)S(1)} %add.125), channel_id=1, replica_groups=mesh['site'=16,'y'=4,'x'=4,'core'=2] {'y','x'}, dimensions={0} | all-to-all | bytes 1572864 | tf_op jit(solution)/shard_map/all_to_all | solution.py:156
  59.7 0.6 %maximum_bitcast_fusion = f32[1,2,96,128]{3,2,1,0:T(8,128)} fusion(f32[1,96,128]{2,1,0:T(8,128)S(1)} %bitcast.9, f32[1,96,128]{2,1,0:T(8,128)S(1)} %bitcast.8), kind=kLoop, calls=%fused_computation | loop fusion | flops 24576 | bytes 196608 | tf_op jit(solution)/shard_map/broadcast_in_dim | solution.py:169
  (2 shorter events, 0.1 us)
Async XLA Ops:
  3.5 4.2 %collective-permute-start = (f32[16,96,128]{2,1,0:T(8,128)S(1)}, f32[16,96,128]{2,1,0:T(8,128)S(1)}, u32[]{:S(2)}, u32[]{:S(2)}) collective-permute-start(f32[16,96,128]{2,1,0:T(8,128)S(1)} %get-tuple-element.12), channel_id=1, source_target_pairs={{0,1},{1,0},{2,3},{3,2},{4,5},{5,4},{6,7},{7,6},{8,9},{9,8},{10,11... | collective-permute-start | bytes 2359304 | tf_op jit(solution)/shard_map/ppermute | solution.py:155
  29.3 7.2 %collective-permute-start.1 = (f32[96,128]{1,0:T(8,128)S(1)}, f32[96,128]{1,0:T(8,128)S(1)}, u32[]{:S(2)}, u32[]{:S(2)}) collective-permute-start(f32[96,128]{1,0:T(8,128)S(1)} %fusion.1), channel_id=1, source_target_pairs={{0,32},{32,64},{64,96},{96,128},{128,160},{160,192},{192,224},{224... | collective-permute-start | bytes 147464 | tf_op jit(solution)/shard_map/ppermute | solution.py:166
  32.2 4.2 %copy-start = (f32[1,96,128]{2,1,0:T(8,128)S(1)}, f32[1,96,128]{2,1,0:T(8,128)}, u32[]{:S(2)}) copy-start(f32[1,96,128]{2,1,0:T(8,128)} %fresh_ref.1) | copy-start | bytes 147460
  37.8 4.2 %collective-permute-start.2 = (f32[16,96,128]{2,1,0:T(8,128)S(1)}, f32[16,96,128]{2,1,0:T(8,128)S(1)}, u32[]{:S(2)}, u32[]{:S(2)}) collective-permute-start(f32[16,96,128]{2,1,0:T(8,128)S(1)} %get-tuple-element.16), channel_id=1, source_target_pairs={{0,1},{1,0},{2,3},{3,2},{4,5},{5,4},{6,7},{7,6},{8,9},{9,8},{10,11... | collective-permute-start | bytes 2359304 | tf_op jit(solution)/shard_map/ppermute | solution.py:155

commit v6 on v5

--- a/solution.py
+++ b/solution.py
@@ -151,22 +151,45 @@
     )(selected, fresh, passed, both)
 
 
-def scatter_sum(kept, sent):
+def last_kernel(earlier_ref, arrived_ref, out_hbm, total_ref, sem):
+    first = pltpu.make_async_copy(earlier_ref, out_hbm.at[0, 0], sem.at[0])
+    first.start()
+    total = arrived_ref[0]
+    for chip in range(1, arrived_ref.shape[0]):
+        total = total + arrived_ref[chip]
+    total_ref[...] = total
+    second = pltpu.make_async_copy(total_ref, out_hbm.at[0, 1], sem.at[1])
+    second.start()
+    first.wait()
+    second.wait()
+
+
+def last_sum(earlier, arrived):
+    rows, samples = earlier.shape
+    return pl.pallas_call(
+        last_kernel,
+        out_shape=jax.ShapeDtypeStruct((1, TICKS, rows, samples), earlier.dtype),
+        in_specs=[VMEM] * 2,
+        out_specs=HBM,
+        scratch_shapes=[pltpu.VMEM(earlier.shape, earlier.dtype), pltpu.SemaphoreType.DMA((2,))],
+        compiler_params=pltpu.CompilerParams(vmem_limit_bytes=4 * 1024 * 1024),
+        name="last_sum",
+    )(earlier, arrived)
+
+
+def scatter(kept, sent):
     paired = kept + lax.ppermute(sent, "core", [(0, 1), (1, 0)])
-    arrived = lax.all_to_all(paired, CHIPS, 0, 0, tiled=True)
-    total = functools.reduce(jnp.add, [arrived[chip] for chip in range(arrived.shape[0])])
-    return lax.optimization_barrier(total)
+    return lax.all_to_all(paired, CHIPS, 0, 0, tiled=True)
 
 
 def on_device(site_tensor, panels, fresh, outcomes):
     sites = lax.axis_size("site")
     kept, sent, tensor, selected = first_product(outcomes, panels, site_tensor)
-    results = [scatter_sum(kept, sent)]
-    for tick in range(1, TICKS):
-        passed = lax.ppermute(results[-1], "site", [(i, i + 1) for i in range(sites - 1)])
-        both = tensor_halves(tensor)
-        results.append(scatter_sum(*later_product(tick, selected, fresh, passed, both)))
-    return jnp.stack(results, 0)[None]
+    arrived = scatter(kept, sent)
+    earlier = functools.reduce(jnp.add, [arrived[chip] for chip in range(arrived.shape[0])])
+    passed = lax.ppermute(earlier, "site", [(i, i + 1) for i in range(sites - 1)])
+    both = tensor_halves(tensor)
+    return last_sum(earlier, scatter(*later_product(1, selected, fresh, passed, both)))
 
 
 def solution(mesh):

time: 60.7 us -> 60.6 us (level)
  the two profiles are of different devices: /device:TPU:384 before, /device:TPU:128 now
where the time goes in v6:
time: 60.6 us; the launch traced here: 60.3 us
  blocking collectives  39 us (64%)
  starting transfers between devices  7.67 us (13%)
  waiting for transfers between devices  7.19 us (12%)
  Pallas kernels  6.17 us (10%)
    all_to_all x2, blocking collectives, scatter(): return lax.all_to_all(paired, CHIPS, 0, 0, tiled=True)  39 us
    ppermute x2, waiting for transfers between devices, scatter(): paired = kept + lax.ppermute(sent, 'core', [(0, 1), (1, 0)])  4.5 us
    ppermute x2, starting transfers between devices, scatter(): paired = kept + lax.ppermute(sent, 'core', [(0, 1), (1, 0)])  3.84 us
    ppermute x1, starting transfers between devices, on_device(): lax.ppermute(earlier, 'site', [(i, i + 1) for i in range(sites - 1)])  3.83 us
    pallas_call x1, Pallas kernels, first_product(): pl.pallas_call(first_kernel, out_shape=[block, block, whole, pltpu.VMEM(o...  3.48 us
    ppermute x1, waiting for transfers between devices, on_device(): lax.ppermute(earlier, 'site', [(i, i + 1) for i in range(sites - 1)])  2.69 us
    pallas_call x1, Pallas kernels, later_product(): pl.pallas_call(functools.partial(later_kernel, tick), out_shape=[block, b...  1.36 us
  transfers between devices with their start and end apart: 3, of which 3 were waited for; matrix products, arithmetic and copies ran while one was open for 0% of the time, Pallas kernels for 1%

profile of v6, /device:TPU:128, one launch (start us, length us, event | category | flops | bytes accessed | tf_op | source)
XLA Modules:
  0.0 60.3 jit_solution(4255267887702883072)
XLA Ops:
  0.0 3.5 %first_product.1 = (f32[16,96,128]{2,1,0:T(8,128)S(1)}, f32[16,96,128]{2,1,0:T(8,128)S(1)}, f32[4,96,3072]{2,1,0:T(8,128)S(1)}, s32[1,2,128]{2,1,0:T(2,128)S(1)}) custom-call(s32[1,2,128]{2,1,0:T(2,128)} %selected_hbm.1, f32[1,96,128]{2,1,0:T(8,128)} %vectors_hbm.1, f32[1,4,96,3072]{3,2,1,0:T(8,128)} %tensor_hbm.1), custom_call_target="tpu_custom_call" | custom-call | flops 905969664 | bytes 4718592 | tf_op jit(solution)/shard_map/first_product/pallas_call | solution.py:110
  3.5 1.9 %collective-permute-start = (f32[16,96,128]{2,1,0:T(8,128)S(1)}, f32[16,96,128]{2,1,0:T(8,128)S(1)}, u32[]{:S(2)}, u32[]{:S(2)}) collective-permute-start(f32[16,96,128]{2,1,0:T(8,128)S(1)} %get-tuple-element.12), channel_id=1, source_target_pairs={{0,1},{1,0},{2,3},{3,2},{4,5},{5,4},{6,7},{7,6},{8,9},{9,8},{10,11... | collective-permute-start | bytes 2359304 | tf_op jit(solution)/shard_map/ppermute | solution.py:181
  5.4 2.3 %collective-permute-done = f32[16,96,128]{2,1,0:T(8,128)S(1)} collective-permute-done((f32[16,96,128]{2,1,0:T(8,128)S(1)}, f32[16,96,128]{2,1,0:T(8,128)S(1)}, u32[]{:S(2)}, u32[]{:S(2)}) %collective-permute-start) | collective-permute-done | bytes 786464 | tf_op jit(solution)/shard_map/ppermute | solution.py:181
  7.7 0.1 add.57
  7.8 21.5 %all_to_all.10 = f32[16,96,128]{2,1,0:T(8,128)S(1)} all-to-all(f32[16,96,128]{2,1,0:T(8,128)S(1)} %add.57), channel_id=1, replica_groups=mesh['site'=16,'y'=4,'x'=4,'core'=2] {'y','x'}, dimensions={0} | all-to-all | bytes 1572864 | tf_op jit(solution)/shard_map/all_to_all | solution.py:182
  29.3 3.8 %collective-permute-start.1 = (f32[96,128]{1,0:T(8,128)S(1)}, f32[96,128]{1,0:T(8,128)S(1)}, u32[]{:S(2)}, u32[]{:S(2)}) collective-permute-start(f32[96,128]{1,0:T(8,128)S(1)} %fusion.earlier_ref), channel_id=1, source_target_pairs={{0,32},{32,64},{64,96},{96,128},{128,160},{160,192},{192,224},{224... | collective-permute-start | bytes 147464 | tf_op jit(solution)/shard_map/ppermute | solution.py:190
  33.1 0.0 copy-start
  33.1 0.7 %tensor_halves.1.halves_ref = bf16[768,3072]{1,0:T(8,128)(2,1)S(1)} custom-call(f32[4,96,3072]{2,1,0:T(8,128)S(1)} %get-tuple-element.14.tensor_ref), custom_call_target="tpu_custom_call" | custom-call | flops 905969664 | tf_op jit(solution)/shard_map/tensor_halves/pallas_call | solution.py:128
  33.8 2.7 %collective-permute-done.1.passed_ref = f32[96,128]{1,0:T(8,128)S(1)} collective-permute-done((f32[96,128]{1,0:T(8,128)S(1)}, f32[96,128]{1,0:T(8,128)S(1)}, u32[]{:S(2)}, u32[]{:S(2)}) %collective-permute-start.1) | collective-permute-done | bytes 49184 | tf_op jit(solution)/shard_map/ppermute | solution.py:190
  36.5 0.0 copy-done
  36.5 1.4 %later_product.1 = (f32[16,96,128]{2,1,0:T(8,128)S(1)}, f32[16,96,128]{2,1,0:T(8,128)S(1)}) custom-call(s32[1,2,128]{2,1,0:T(2,128)S(1)} %get-tuple-element.13.selected_ref, f32[1,96,128]{2,1,0:T(8,128)S(1)} %copy-done, f32[96,128]{1,0:T(8,128)S(1)} %collective-permute-done.1.passed_ref, bf16[768,3072]{1,0:T(8,128)(2,1)S(1)} %tensor_halves.1.halves_ref), custom_call_target="tpu_custom_call" | custom-call | flops 905969664 | bytes 1572864 | tf_op jit(solution)/shard_map/later_product/pallas_call | solution.py:143
  37.8 1.9 %collective-permute-start.2 = (f32[16,96,128]{2,1,0:T(8,128)S(1)}, f32[16,96,128]{2,1,0:T(8,128)S(1)}, u32[]{:S(2)}, u32[]{:S(2)}) collective-permute-start(f32[16,96,128]{2,1,0:T(8,128)S(1)} %get-tuple-element.16), channel_id=1, source_target_pairs={{0,1},{1,0},{2,3},{3,2},{4,5},{5,4},{6,7},{7,6},{8,9},{9,8},{10,11... | collective-permute-start | bytes 2359304 | tf_op jit(solution)/shard_map/ppermute | solution.py:181
  39.8 2.3 %collective-permute-done.2 = f32[16,96,128]{2,1,0:T(8,128)S(1)} collective-permute-done((f32[16,96,128]{2,1,0:T(8,128)S(1)}, f32[16,96,128]{2,1,0:T(8,128)S(1)}, u32[]{:S(2)}, u32[]{:S(2)}) %collective-permute-start.2) | collective-permute-done | bytes 786464 | tf_op jit(solution)/shard_map/ppermute | solution.py:181
  42.0 0.1 add.74
  42.1 17.5 %all_to_all.11.arrived_ref = f32[16,96,128]{2,1,0:T(8,128)S(1)} all-to-all(f32[16,96,128]{2,1,0:T(8,128)S(1)} %add.74), channel_id=1, replica_groups=mesh['site'=16,'y'=4,'x'=4,'core'=2] {'y','x'}, dimensions={0} | all-to-all | bytes 1572864 | tf_op jit(solution)/shard_map/all_to_all | solution.py:182
  59.7 0.7 %last_sum.1 = f32[1,2,96,128]{3,2,1,0:T(8,128)} custom-call(f32[96,128]{1,0:T(8,128)S(1)} %fusion.earlier_ref, f32[16,96,128]{2,1,0:T(8,128)S(1)} %all_to_all.11.arrived_ref), custom_call_target="tpu_custom_call" | custom-call | tf_op jit(solution)/shard_map/last_sum/pallas_call | solution.py:169
  (1 shorter events, 0.0 us)
Async XLA Ops:
  3.5 4.2 %collective-permute-start = (f32[16,96,128]{2,1,0:T(8,128)S(1)}, f32[16,96,128]{2,1,0:T(8,128)S(1)}, u32[]{:S(2)}, u32[]{:S(2)}) collective-permute-start(f32[16,96,128]{2,1,0:T(8,128)S(1)} %get-tuple-element.12), channel_id=1, source_target_pairs={{0,1},{1,0},{2,3},{3,2},{4,5},{5,4},{6,7},{7,6},{8,9},{9,8},{10,11... | collective-permute-start | bytes 2359304 | tf_op jit(solution)/shard_map/ppermute | solution.py:181
  29.3 7.2 %collective-permute-start.1 = (f32[96,128]{1,0:T(8,128)S(1)}, f32[96,128]{1,0:T(8,128)S(1)}, u32[]{:S(2)}, u32[]{:S(2)}) collective-permute-start(f32[96,128]{1,0:T(8,128)S(1)} %fusion.earlier_ref), channel_id=1, source_target_pairs={{0,32},{32,64},{64,96},{96,128},{128,160},{160,192},{192,224},{224... | collective-permute-start | bytes 147464 | tf_op jit(solution)/shard_map/ppermute | solution.py:190
  33.1 3.4 %copy-start = (f32[1,96,128]{2,1,0:T(8,128)S(1)}, f32[1,96,128]{2,1,0:T(8,128)}, u32[]{:S(2)}) copy-start(f32[1,96,128]{2,1,0:T(8,128)} %fresh_ref.1) | copy-start | bytes 147460
  37.8 4.2 %collective-permute-start.2 = (f32[16,96,128]{2,1,0:T(8,128)S(1)}, f32[16,96,128]{2,1,0:T(8,128)S(1)}, u32[]{:S(2)}, u32[]{:S(2)}) collective-permute-start(f32[16,96,128]{2,1,0:T(8,128)S(1)} %get-tuple-element.16), channel_id=1, source_target_pairs={{0,1},{1,0},{2,3},{3,2},{4,5},{5,4},{6,7},{7,6},{8,9},{9,8},{10,11... | collective-permute-start | bytes 2359304 | tf_op jit(solution)/shard_map/ppermute | solution.py:181
